TPU v7x, 32 devices: a whole 2x2x4 slice. The times are simulated.
32 devices in a mesh: dp: 4 (over z), section: 4 (over y, x), expert: 2 (over core).
Axes of the slice: x: 2, y: 2, z: 4, core: 2. Of those that a mesh axis runs over, the one named last changes fastest.
Arguments:
- tokens: bfloat16 [1024, 5120], P(('dp', 'expert')), may hold values from -6 to 6
- cotangent: bfloat16 [1024, 5120], P(('dp', 'expert')), may hold values from -6 to 6
- norm_gain: float32 [4, 5120], P('section'), may hold values from 0.25 to 1.75
- route_gates: float32 [4, 1024, 6], P('section', ('dp', 'expert')), may hold values from 0.5 to 2
- expert_ids: int32 [4, 1024, 6], P('section', ('dp', 'expert')), may hold values from 0 to 159, as said below
- expert_map: int32 [4, 2], P('section'), may hold values from 0 to 1, each once within a row
- w_gate: bfloat16 [4, 2, 5120, 768], P('section', 'expert', 'dp'), may hold values from -0.078125 to 0.078125
- w_up: bfloat16 [4, 2, 5120, 768], P('section', 'expert', 'dp'), may hold values from -0.078125 to 0.078125
- w_down: bfloat16 [4, 2, 768, 5120], P('section', 'expert', None, 'dp'), may hold values from -0.21875 to 0.21875
Outputs:
- layer_out: bfloat16 [4, 1024, 5120], P('section', ('dp', 'expert'))
- input_grad: bfloat16 [4, 1024, 5120], P('section', ('dp', 'expert'))
- grad_gate: bfloat16 [4, 2, 5120, 768], P('section', 'expert', 'dp')
- grad_up: bfloat16 [4, 2, 5120, 768], P('section', 'expert', 'dp')
- grad_down: bfloat16 [4, 2, 768, 5120], P('section', 'expert', None, 'dp')
Inputs may be any that keep to these rules, and one draw needn't show every extreme that they name: `expert_ids`: each token names 6 different experts on each layer. The held experts are those below 2. Split the 128 tokens of one index pair of dp and expert in order into 4 equal blocks: in each block each held expert is named by at most 2 tokens, and on every layer one held expert is named by exactly 2 tokens of every block, so by 8 tokens of every such pair. `expert_map`: each layer's row names every held expert once.
All inputs are finite; a program needn't handle non-finite values.
Results may differ from a plain program's by a relative error of at most 0.03.
Values may be sent and summed in bfloat16 or wider, within the bound.
A program may use at most 128 MiB of HBM per device.

v0:
```python
import jax
import jax.numpy as jnp
from jax import lax
from jax.sharding import PartitionSpec as P

CAP = 8


def from_behind(value, axis, steps):
    count = lax.axis_size(axis)
    leading, last = (max(0, -steps), min(count, count - steps))
    return lax.ppermute(value, axis, [(source, source + steps) for source in range(leading, last)])


def route_tables(route_ids, route_weights, held_experts, capacity):
    matches = route_ids[:, :, None] == held_experts[None, None, :]
    chosen = jnp.any(matches, axis=1)
    weights = jnp.sum(jnp.where(matches, route_weights[:, :, None], 0.0), axis=1)
    position = jnp.cumsum(chosen.astype(jnp.int32), axis=0) - 1
    slot_ids = jnp.arange(capacity, dtype=jnp.int32)
    placed = chosen[:, :, None] & (position[:, :, None] == slot_ids[None, None, :])
    return (placed.astype(jnp.bfloat16), weights)


def deliver(buffer):
    flat_buffer = buffer.reshape((-1,) + buffer.shape[2:])
    exchanged = lax.all_to_all(
        flat_buffer, ("dp", "expert"), split_axis=0, concat_axis=0, tiled=True
    )
    return exchanged.reshape(buffer.shape)


def gate_backward(hidden_grad, gate_pre, up_pre):
    sigmoid_gate = jax.nn.sigmoid(gate_pre)
    gate_grad = (
        hidden_grad * up_pre * sigmoid_gate * (1.0 + gate_pre * (1.0 - sigmoid_gate))
    ).astype(jnp.bfloat16)
    up_grad = (hidden_grad * gate_pre * sigmoid_gate).astype(jnp.bfloat16)
    return (gate_grad, up_grad)


def local(tokens, cotangent, norm_gain, route_gates, expert_ids, expert_map, w_gate, w_up, w_down):
    section_index = lax.axis_index("section")
    section_count = lax.axis_size("section")
    dp_groups = lax.axis_size("dp")
    held_experts = expert_map[0]
    route_rows = expert_ids[0]
    gate_rows = route_gates[0]
    norm_scale = norm_gain[0][None, :]
    gate_weight = w_gate[0, 0]
    up_weight = w_up[0, 0]
    down_weight = w_down[0, 0]
    model_width = tokens.shape[1]
    slice_width = gate_weight.shape[0]
    contract_first = (((0,), (0,)), ((), ()))
    contract_second = (((1,), (1,)), ((), ()))
    dispatch, token_weight = route_tables(route_rows, gate_rows, held_experts, CAP)
    current = tokens
    stored = None
    for step_index in range(section_count):
        forward_rows_here = current.shape[0]
        forward_wide_in = current.astype(jnp.float32)
        forward_inv_rms = lax.rsqrt(
            jnp.mean(forward_wide_in * forward_wide_in, axis=1, keepdims=True) + 1e-06
        )
        normed = (forward_wide_in * forward_inv_rms * norm_scale).astype(jnp.bfloat16)
        forward_outgoing = jnp.einsum(
            "tpc,tqd->qpcd",
            dispatch,
            normed.reshape(forward_rows_here, dp_groups, slice_width),
            preferred_element_type=jnp.float32,
        ).astype(jnp.bfloat16)
        forward_slot_rows = deliver(forward_outgoing).reshape(-1, slice_width)
        gate_part = jnp.dot(forward_slot_rows, gate_weight, preferred_element_type=jnp.float32)
        up_part = jnp.dot(forward_slot_rows, up_weight, preferred_element_type=jnp.float32)
        forward_gate_pre = lax.psum(gate_part.astype(jnp.bfloat16), "dp").astype(jnp.float32)
        forward_up_pre = lax.psum(up_part.astype(jnp.bfloat16), "dp").astype(jnp.float32)
        forward_activated = (
            forward_gate_pre * jax.nn.sigmoid(forward_gate_pre) * forward_up_pre
        ).astype(jnp.bfloat16)
        expert_out = jnp.dot(
            forward_activated, down_weight, preferred_element_type=jnp.float32
        ).astype(jnp.bfloat16)
        forward_returned = deliver(expert_out.reshape(forward_outgoing.shape))
        picked = jnp.einsum(
            "tpc,qpcd->tpqd", dispatch, forward_returned, preferred_element_type=jnp.bfloat16
        )
        combined = jnp.sum(
            token_weight[:, :, None, None] * picked.astype(jnp.float32), axis=1
        ).reshape(forward_rows_here, model_width)
        result = (forward_wide_in + combined).astype(jnp.bfloat16)
        result, saved_state = (
            result,
            (
                current,
                forward_inv_rms,
                forward_slot_rows,
                forward_gate_pre,
                forward_up_pre,
                forward_activated,
            ),
        )
        if step_index == 0:
            stored = (result, saved_state)
        else:
            stored = jax.tree.map(
                lambda latest, earlier: jnp.where(section_index == step_index, latest, earlier),
                (result, saved_state),
                stored,
            )
        if step_index + 1 < section_count:
            current = from_behind(result, "section", 1)
    layer_result, saved_state = stored
    incoming = cotangent
    collected = None
    for step_index in range(section_count):
        layer_in, inv_rms, slot_rows, gate_pre, up_pre, activated = saved_state
        rows_here = incoming.shape[0]
        experts_here = dispatch.shape[1]
        grad_wide = incoming.astype(jnp.float32)
        scaled = (token_weight[:, :, None] * grad_wide[:, None, :]).astype(jnp.bfloat16)
        scaled = scaled.reshape(rows_here, experts_here, dp_groups, slice_width)
        outgoing = jnp.einsum(
            "tpc,tpqd->qpcd", dispatch, scaled, preferred_element_type=jnp.bfloat16
        )
        slot_grad = deliver(outgoing).reshape(-1, slice_width)
        backward_down_grad = lax.dot_general(
            activated, slot_grad, contract_first, preferred_element_type=jnp.float32
        )
        hidden_part = lax.dot_general(
            slot_grad, down_weight, contract_second, preferred_element_type=jnp.float32
        )
        hidden_grad = lax.psum(hidden_part.astype(jnp.bfloat16), "dp").astype(jnp.float32)
        gate_grad, up_grad = gate_backward(hidden_grad, gate_pre, up_pre)
        backward_gate_wgrad = lax.dot_general(
            slot_rows, gate_grad, contract_first, preferred_element_type=jnp.float32
        )
        backward_up_wgrad = lax.dot_general(
            slot_rows, up_grad, contract_first, preferred_element_type=jnp.float32
        )
        slot_back = (
            lax.dot_general(
                gate_grad, gate_weight, contract_second, preferred_element_type=jnp.float32
            )
            + lax.dot_general(
                up_grad, up_weight, contract_second, preferred_element_type=jnp.float32
            )
        ).astype(jnp.bfloat16)
        returned = deliver(slot_back.reshape(outgoing.shape))
        normed_grad = jnp.einsum(
            "tpc,qpcd->tqd", dispatch, returned, preferred_element_type=jnp.float32
        ).reshape(rows_here, model_width)
        wide_in = layer_in.astype(jnp.float32)
        scaled_grad = normed_grad * norm_scale
        through_norm = inv_rms * (
            scaled_grad
            - wide_in * inv_rms * inv_rms * jnp.mean(scaled_grad * wide_in, axis=1, keepdims=True)
        )
        grad_in = (grad_wide + through_norm).astype(jnp.bfloat16)
        weight_grads = (backward_gate_wgrad, backward_up_wgrad, backward_down_grad)
        if step_index == 0:
            collected = (grad_in, weight_grads)
        else:
            collected = jax.tree.map(
                lambda latest, earlier: jnp.where(
                    section_index == section_count - 1 - step_index, latest, earlier
                ),
                (grad_in, weight_grads),
                collected,
            )
        if step_index + 1 < section_count:
            incoming = from_behind(grad_in, "section", -1)
    grad_in, weight_grads = collected
    gate_wgrad, up_wgrad, down_grad = weight_grads
    return (
        layer_result[None],
        grad_in[None],
        gate_wgrad.astype(jnp.bfloat16)[None, None],
        up_wgrad.astype(jnp.bfloat16)[None, None],
        down_grad.astype(jnp.bfloat16)[None, None],
    )


def solution(mesh):
    return jax.shard_map(
        local,
        mesh=mesh,
        in_specs=(
            P(("dp", "expert"), None),
            P(("dp", "expert"), None),
            P("section", None),
            P("section", ("dp", "expert"), None),
            P("section", ("dp", "expert"), None),
            P("section", None),
            P("section", "expert", "dp", None),
            P("section", "expert", "dp", None),
            P("section", "expert", None, "dp"),
        ),
        out_specs=(
            P("section", ("dp", "expert"), None),
            P("section", ("dp", "expert"), None),
            P("section", "expert", "dp", None),
            P("section", "expert", "dp", None),
            P("section", "expert", None, "dp"),
        ),
        check_vma=False,
    )
```

profile of v0, /device:TPU:0, one launch (start us, length us, event | category | flops | bytes accessed | tf_op | source)
XLA Modules:
  0.0 742.3 jit_solution(14900021208772421343)
XLA Ops:
  17.9 13.4 %all_to_all.80 = bf16[8,8,1280]{2,1,0:T(8,128)(2,1)S(1)} all-to-all(bf16[8,8,1280]{2,1,0:T(8,128)(2,1)S(1)} %bitcast.319), channel_id=1, replica_groups=mesh['dp'=4,'section'=4,'expert'=2] {'dp','expert'}, dimensions={0} | all-to-all | bytes 327680 | tf_op jit(solution)/shard_map/all_to_all | solution.py:27
  35.1 34.4 %all-reduce.24.cloned.1.call-done = (bf16[64,768]{1,0:T(8,128)(2,1)}, bf16[64,768]{1,0:T(8,128)(2,1)}) async-done(((bf16[64,768]{1,0:T(8,128)(2,1)}, bf16[64,768]{1,0:T(8,128)(2,1)}), (bf16[64,768]{1,0:T(8,128)(2,1)}, bf16[64,768]{1,0:T(8,128)(2,1)})) %all-reduce.24.cloned.1.call-update) | async-done | bytes 196624 | tf_op jit(solution)/shard_map/psum | solution.py:77
  75.3 7.1 all-to-all-done.1
  93.6 27.4 %collective-permute-done = bf16[128,5120]{1,0:T(8,128)(2,1)S(1)} collective-permute-done((bf16[128,5120]{1,0:T(8,128)(2,1)S(1)}, bf16[128,5120]{1,0:T(8,128)(2,1)S(1)}, u32[]{:S(2)}, u32[]{:S(2)}) %collective-permute-start) | collective-permute-done | bytes 1310752 | tf_op jit(solution)/shard_map/ppermute | solution.py:12
  128.2 10.7 %all_to_all.81 = bf16[8,8,1280]{2,1,0:T(8,128)(2,1)S(1)} all-to-all(bf16[8,8,1280]{2,1,0:T(8,128)(2,1)S(1)} %bitcast.320), channel_id=1, replica_groups=mesh['dp'=4,'section'=4,'expert'=2] {'dp','expert'}, dimensions={0} | all-to-all | bytes 327680 | tf_op jit(solution)/shard_map/all_to_all | solution.py:27
  142.8 35.3 %all-reduce.22.cloned.1.call-done = (bf16[64,768]{1,0:T(8,128)(2,1)}, bf16[64,768]{1,0:T(8,128)(2,1)}) async-done(((bf16[64,768]{1,0:T(8,128)(2,1)}, bf16[64,768]{1,0:T(8,128)(2,1)}), (bf16[64,768]{1,0:T(8,128)(2,1)}, bf16[64,768]{1,0:T(8,128)(2,1)})) %all-reduce.22.cloned.1.call-update) | async-done | bytes 196624 | tf_op jit(solution)/shard_map/psum | solution.py:77
  179.6 10.5 %all_to_all.82 = bf16[8,8,1280]{2,1,0:T(8,128)(2,1)S(1)} all-to-all(bf16[8,8,1280]{2,1,0:T(8,128)(2,1)S(1)} %fusion.72), channel_id=1, replica_groups=mesh['dp'=4,'section'=4,'expert'=2] {'dp','expert'}, dimensions={0} | all-to-all | bytes 327680 | tf_op jit(solution)/shard_map/all_to_all | solution.py:27
  201.5 27.2 %collective-permute-done.1 = bf16[128,5120]{1,0:T(8,128)(2,1)S(1)} collective-permute-done((bf16[128,5120]{1,0:T(8,128)(2,1)S(1)}, bf16[128,5120]{1,0:T(8,128)(2,1)S(1)}, u32[]{:S(2)}, u32[]{:S(2)}) %collective-permute-start.1) | collective-permute-done | bytes 1310752 | tf_op jit(solution)/shard_map/ppermute | solution.py:12
  235.9 10.7 %all_to_all.83 = bf16[8,8,1280]{2,1,0:T(8,128)(2,1)S(1)} all-to-all(bf16[8,8,1280]{2,1,0:T(8,128)(2,1)S(1)} %bitcast.321), channel_id=1, replica_groups=mesh['dp'=4,'section'=4,'expert'=2] {'dp','expert'}, dimensions={0} | all-to-all | bytes 327680 | tf_op jit(solution)/shard_map/all_to_all | solution.py:27
  250.5 35.4 %all-reduce.20.cloned.1.call-done = (bf16[64,768]{1,0:T(8,128)(2,1)}, bf16[64,768]{1,0:T(8,128)(2,1)}) async-done(((bf16[64,768]{1,0:T(8,128)(2,1)}, bf16[64,768]{1,0:T(8,128)(2,1)}), (bf16[64,768]{1,0:T(8,128)(2,1)}, bf16[64,768]{1,0:T(8,128)(2,1)})) %all-reduce.20.cloned.1.call-update) | async-done | bytes 196624 | tf_op jit(solution)/shard_map/psum | solution.py:77
  287.3 10.5 %all_to_all.84 = bf16[8,8,1280]{2,1,0:T(8,128)(2,1)S(1)} all-to-all(bf16[8,8,1280]{2,1,0:T(8,128)(2,1)S(1)} %fusion.73), channel_id=1, replica_groups=mesh['dp'=4,'section'=4,'expert'=2] {'dp','expert'}, dimensions={0} | all-to-all | bytes 327680 | tf_op jit(solution)/shard_map/all_to_all | solution.py:27
  319.6 18.2 %collective-permute-done.2 = bf16[128,5120]{1,0:T(8,128)(2,1)S(1)} collective-permute-done((bf16[128,5120]{1,0:T(8,128)(2,1)}, bf16[128,5120]{1,0:T(8,128)(2,1)S(1)}, u32[]{:S(2)}, u32[]{:S(2)}) %collective-permute-start.2) | collective-permute-done | bytes 1310752 | tf_op jit(solution)/shard_map/ppermute | solution.py:12
  345.6 3.7 all-to-all-start.6
  350.7 5.8 all-to-all-done.6
  360.6 36.6 %all-reduce.18.cloned.1.call-done = (bf16[64,768]{1,0:T(8,128)(2,1)}, bf16[64,768]{1,0:T(8,128)(2,1)}, bf16[64,768]{1,0:T(8,128)(2,1)}) async-done(((bf16[64,768]{1,0:T(8,128)(2,1)}, bf16[64,768]{1,0:T(8,128)(2,1)}, bf16[64,768]{1,0:T(8,128)(2,1)}), (bf16[64,768]{1,0:T(8,128)(2,1)}, bf16[64,768]{1,0:T(8,128)(2,1)}, bf16[64,768]{1,0:T(8,128)(2,1)})) %all-reduce.18.cloned.1.call-update) | async-done | bytes 294928 | tf_op jit(solution)/shard_map/psum | solution.py:77
  402.3 10.3 %all_to_all.85 = bf16[8,8,1280]{2,1,0:T(8,128)(2,1)S(1)} all-to-all(bf16[8,8,1280]{2,1,0:T(8,128)(2,1)S(1)} %fusion.78), channel_id=1, replica_groups=mesh['dp'=4,'section'=4,'expert'=2] {'dp','expert'}, dimensions={0} | all-to-all | bytes 327680 | tf_op jit(solution)/shard_map/all_to_all | solution.py:27
  417.5 30.4 %collective-permute-done.3 = bf16[128,5120]{1,0:T(8,128)(2,1)} collective-permute-done((bf16[128,5120]{1,0:T(8,128)(2,1)S(1)}, bf16[128,5120]{1,0:T(8,128)(2,1)}, u32[]{:S(2)}, u32[]{:S(2)}) %collective-permute-start.3) | collective-permute-done | bytes 1310752 | tf_op jit(solution)/shard_map/ppermute | solution.py:12
  453.3 10.7 %all_to_all.86 = bf16[8,8,1280]{2,1,0:T(8,128)(2,1)S(1)} all-to-all(bf16[8,8,1280]{2,1,0:T(8,128)(2,1)S(1)} %bitcast.313), channel_id=1, replica_groups=mesh['dp'=4,'section'=4,'expert'=2] {'dp','expert'}, dimensions={0} | all-to-all | bytes 327680 | tf_op jit(solution)/shard_map/all_to_all | solution.py:27
  466.1 34.2 %all-reduce.12.cloned.1.call-done = bf16[64,768]{1,0:T(8,128)(2,1)} async-done(((bf16[64,768]{1,0:T(8,128)(2,1)}), bf16[64,768]{1,0:T(8,128)(2,1)}) %all-reduce.12.cloned.1.call-update) | async-done | bytes 98320 | tf_op jit(solution)/shard_map/psum | solution.py:133
  504.6 10.4 %all_to_all.87 = bf16[8,8,1280]{2,1,0:T(8,128)(2,1)S(1)} all-to-all(bf16[8,8,1280]{2,1,0:T(8,128)(2,1)S(1)} %fusion.77), channel_id=1, replica_groups=mesh['dp'=4,'section'=4,'expert'=2] {'dp','expert'}, dimensions={0} | all-to-all | bytes 327680 | tf_op jit(solution)/shard_map/all_to_all | solution.py:27
  522.4 4.0 all-to-all-start.7
  533.6 3.7 fusion.4
  540.6 10.6 %collective-permute-done.4 = bf16[128,5120]{1,0:T(8,128)(2,1)} collective-permute-done((bf16[128,5120]{1,0:T(8,128)(2,1)}, bf16[128,5120]{1,0:T(8,128)(2,1)}, u32[]{:S(2)}, u32[]{:S(2)}) %collective-permute-start.4) | collective-permute-done | bytes 1310752 | tf_op jit(solution)/shard_map/ppermute | solution.py:12
  557.2 4.0 all-to-all-start.12
  561.3 3.9 fusion.126
  573.8 31.5 %all-reduce.14.cloned.1.call-done = bf16[64,768]{1,0:T(8,128)(2,1)} async-done(((bf16[64,768]{1,0:T(8,128)(2,1)}), bf16[64,768]{1,0:T(8,128)(2,1)}) %all-reduce.14.cloned.1.call-update) | async-done | bytes 98320 | tf_op jit(solution)/shard_map/psum | solution.py:133
  610.8 4.3 all-to-all-start.13
  636.4 22.1 %collective-permute-done.5 = bf16[128,5120]{1,0:T(8,128)(2,1)} collective-permute-done((bf16[128,5120]{1,0:T(8,128)(2,1)S(1)}, bf16[128,5120]{1,0:T(8,128)(2,1)}, u32[]{:S(2)}, u32[]{:S(2)}) %collective-permute-start.5) | collective-permute-done | bytes 1310752 | tf_op jit(solution)/shard_map/ppermute | solution.py:12
  664.6 4.0 all-to-all-start.14
  681.1 30.7 %all-reduce.16.cloned.1.call-done = bf16[64,768]{1,0:T(8,128)(2,1)} async-done(((bf16[64,768]{1,0:T(8,128)(2,1)}), bf16[64,768]{1,0:T(8,128)(2,1)}) %all-reduce.16.cloned.1.call-update) | async-done | bytes 98320 | tf_op jit(solution)/shard_map/psum | solution.py:133
  717.4 4.0 all-to-all-start.15
  731.3 3.8 fusion.124
  (258 shorter events, 217.4 us)
Async XLA Ops:
  7.2 62.4 %copy-start = (bf16[1,1,768,1280]{3,2,1,0:T(8,128)(2,1)S(1)}, bf16[1,1,768,1280]{3,2,1,0:T(8,128)(2,1)}, u32[]{:S(2)}) copy-start(bf16[1,1,768,1280]{3,2,1,0:T(8,128)(2,1)} %param.17) | copy-start | bytes 5898244
  7.2 62.3 %all-reduce.24.cloned.1.call-start = ((), (), s32[]{:S(2)}) async-start(), calls=%async_computation.22 | async-start | bytes 393216 | tf_op jit(solution)/shard_map/psum | solution.py:77
  35.1 40.1 %copy-start.59 = (f32[1,128,6]{1,0,2:T(1,128)S(1)}, f32[1,128,6]{1,0,2:T(1,128)}, u32[]{:S(2)}) copy-start(f32[1,128,6]{1,0,2:T(1,128)} %param.12) | copy-start | bytes 9220
  71.6 10.7 %all-to-all-start.1 = ((bf16[8,8,1280]{2,1,0:T(8,128)(2,1)}), bf16[8,8,1280]{2,1,0:T(8,128)(2,1)S(1)}, u32[]{:S(2)}, u32[]{:S(2)}) async-start(bf16[8,8,1280]{2,1,0:T(8,128)(2,1)} %fusion.71), calls=%async_computation.1 | async-start | bytes 327680 | tf_op jit(solution)/shard_map/all_to_all | solution.py:27
  75.1 103.0 %all-reduce.22.cloned.1.call-start = ((), (), s32[]{:S(2)}) async-start(), calls=%async_computation.21 | async-start | bytes 393216 | tf_op jit(solution)/shard_map/psum | solution.py:77
  88.2 33.1 %copy-start.39 = (f32[1,5120]{1,0:T(1,128)S(1)}, f32[1,5120]{1,0:T(1,128)}, u32[]{:S(2)}) copy-start(f32[1,5120]{1,0:T(1,128)} %param.11) | copy-start | bytes 61444
  90.2 30.7 %collective-permute-start = (bf16[128,5120]{1,0:T(8,128)(2,1)S(1)}, bf16[128,5120]{1,0:T(8,128)(2,1)S(1)}, u32[]{:S(2)}, u32[]{:S(2)}) collective-permute-start(bf16[128,5120]{1,0:T(8,128)(2,1)S(1)} %fusion.17), channel_id=1, source_target_pairs={{0,2},{2,4},{4,6},{1,3},{3,5},{5,7},{8,10},{10,12},{12,14},{9,11},... | collective-permute-start | bytes 3932168 | tf_op jit(solution)/shard_map/ppermute | solution.py:12
  121.0 75.0 %copy-start.13 = (bf16[128,5120]{1,0:T(8,128)(2,1)}, bf16[128,5120]{1,0:T(8,128)(2,1)S(1)}, u32[]{:S(2)}) copy-start(bf16[128,5120]{1,0:T(8,128)(2,1)S(1)} %collective-permute-done) | copy-start | bytes 3932164
  142.8 143.1 %all-reduce.20.cloned.1.call-start = ((), (), s32[]{:S(2)}) async-start(), calls=%async_computation.20 | async-start | bytes 393216 | tf_op jit(solution)/shard_map/psum | solution.py:77
  198.0 30.7 %collective-permute-start.1 = (bf16[128,5120]{1,0:T(8,128)(2,1)S(1)}, bf16[128,5120]{1,0:T(8,128)(2,1)S(1)}, u32[]{:S(2)}, u32[]{:S(2)}) collective-permute-start(bf16[128,5120]{1,0:T(8,128)(2,1)S(1)} %fusion.21), channel_id=1, source_target_pairs={{0,2},{2,4},{4,6},{1,3},{3,5},{5,7},{8,10},{10,12},{12,14},{9,11},... | collective-permute-start | bytes 3932168 | tf_op jit(solution)/shard_map/ppermute | solution.py:12
  228.7 75.0 %copy-start.15 = (bf16[128,5120]{1,0:T(8,128)(2,1)}, bf16[128,5120]{1,0:T(8,128)(2,1)S(1)}, u32[]{:S(2)}) copy-start(bf16[128,5120]{1,0:T(8,128)(2,1)S(1)} %collective-permute-done.1) | copy-start | bytes 3932164
  306.8 31.0 %collective-permute-start.2 = (bf16[128,5120]{1,0:T(8,128)(2,1)}, bf16[128,5120]{1,0:T(8,128)(2,1)S(1)}, u32[]{:S(2)}, u32[]{:S(2)}) collective-permute-start(bf16[128,5120]{1,0:T(8,128)(2,1)} %fusion.25), channel_id=1, source_target_pairs={{0,2},{2,4},{4,6},{1,3},{3,5},{5,7},{8,10},{10,12},{12,14},{9,11},... | collective-permute-start | bytes 3932168 | tf_op jit(solution)/shard_map/ppermute | solution.py:12
  316.2 29.4 %all-to-all-start.8 = ((bf16[8,8,1280]{2,1,0:T(8,128)(2,1)}), bf16[8,8,1280]{2,1,0:T(8,128)(2,1)S(1)}, u32[]{:S(2)}, u32[]{:S(2)}) async-start(bf16[8,8,1280]{2,1,0:T(8,128)(2,1)} %bitcast.309), calls=%async_computation.8 | async-start | bytes 327680 | tf_op jit(solution)/shard_map/all_to_all | solution.py:27
  345.6 10.9 %all-to-all-start.6 = ((bf16[8,8,1280]{2,1,0:T(8,128)(2,1)}), bf16[8,8,1280]{2,1,0:T(8,128)(2,1)S(1)}, u32[]{:S(2)}, u32[]{:S(2)}) async-start(bf16[8,8,1280]{2,1,0:T(8,128)(2,1)} %bitcast.34), calls=%async_computation.6 | async-start | bytes 327680 | tf_op jit(solution)/shard_map/all_to_all | solution.py:27
  349.3 47.8 %all-reduce.18.cloned.1.call-start = ((), (), s32[]{:S(2)}) async-start(), calls=%async_computation.19 | async-start | bytes 589824 | tf_op jit(solution)/shard_map/psum | solution.py:77
  350.7 46.4 %copy-start.43 = (bf16[64,768]{1,0:T(8,128)(2,1)S(1)}, bf16[64,768]{1,0:T(8,128)(2,1)}, u32[]{:S(2)}) copy-start(bf16[64,768]{1,0:T(8,128)(2,1)} %get-tuple-element.12) | copy-start | bytes 294916
  350.7 46.4 %copy-start.44 = (bf16[64,768]{1,0:T(8,128)(2,1)S(1)}, bf16[64,768]{1,0:T(8,128)(2,1)}, u32[]{:S(2)}) copy-start(bf16[64,768]{1,0:T(8,128)(2,1)} %get-tuple-element.13) | copy-start | bytes 294916
  356.5 40.6 %copy-start.45 = (bf16[64,768]{1,0:T(8,128)(2,1)S(1)}, bf16[64,768]{1,0:T(8,128)(2,1)}, u32[]{:S(2)}) copy-start(bf16[64,768]{1,0:T(8,128)(2,1)} %get-tuple-element.10) | copy-start | bytes 294916
  356.5 40.6 %copy-start.46 = (bf16[64,768]{1,0:T(8,128)(2,1)S(1)}, bf16[64,768]{1,0:T(8,128)(2,1)}, u32[]{:S(2)}) copy-start(bf16[64,768]{1,0:T(8,128)(2,1)} %get-tuple-element.11) | copy-start | bytes 294916
  356.5 40.6 %copy-start.47 = (bf16[64,768]{1,0:T(8,128)(2,1)S(1)}, bf16[64,768]{1,0:T(8,128)(2,1)}, u32[]{:S(2)}) copy-start(bf16[64,768]{1,0:T(8,128)(2,1)} %get-tuple-element.8) | copy-start | bytes 294916
  356.5 40.6 %copy-start.48 = (bf16[64,768]{1,0:T(8,128)(2,1)S(1)}, bf16[64,768]{1,0:T(8,128)(2,1)}, u32[]{:S(2)}) copy-start(bf16[64,768]{1,0:T(8,128)(2,1)} %get-tuple-element.9) | copy-start | bytes 294916
  360.5 139.8 %all-reduce.12.cloned.1.call-start = ((), (), s32[]{:S(2)}) async-start(), calls=%async_computation.16 | async-start | bytes 196608 | tf_op jit(solution)/shard_map/psum | solution.py:133
  416.0 31.9 %collective-permute-start.3 = (bf16[128,5120]{1,0:T(8,128)(2,1)S(1)}, bf16[128,5120]{1,0:T(8,128)(2,1)}, u32[]{:S(2)}, u32[]{:S(2)}) collective-permute-start(bf16[128,5120]{1,0:T(8,128)(2,1)S(1)} %fusion.39), channel_id=1, source_target_pairs={{2,0},{4,2},{6,4},{3,1},{5,3},{7,5},{10,8},{12,10},{14,12},{11,9},... | collective-permute-start | bytes 3932168 | tf_op jit(solution)/shard_map/ppermute | solution.py:12
  519.0 32.2 %collective-permute-start.4 = (bf16[128,5120]{1,0:T(8,128)(2,1)}, bf16[128,5120]{1,0:T(8,128)(2,1)}, u32[]{:S(2)}, u32[]{:S(2)}) collective-permute-start(bf16[128,5120]{1,0:T(8,128)(2,1)} %fusion.43), channel_id=1, source_target_pairs={{2,0},{4,2},{6,4},{3,1},{5,3},{7,5},{10,8},{12,10},{14,12},{11,9},... | collective-permute-start | bytes 3932168 | tf_op jit(solution)/shard_map/ppermute | solution.py:12
  522.4 11.3 %all-to-all-start.7 = ((bf16[8,8,1280]{2,1,0:T(8,128)(2,1)}), bf16[8,8,1280]{2,1,0:T(8,128)(2,1)}, u32[]{:S(2)}, u32[]{:S(2)}) async-start(bf16[8,8,1280]{2,1,0:T(8,128)(2,1)} %fusion.74), calls=%async_computation.7 | async-start | bytes 327680 | tf_op jit(solution)/shard_map/all_to_all | solution.py:27
  557.2 11.3 %all-to-all-start.12 = ((bf16[8,8,1280]{2,1,0:T(8,128)(2,1)}), bf16[8,8,1280]{2,1,0:T(8,128)(2,1)}, u32[]{:S(2)}, u32[]{:S(2)}) async-start(bf16[8,8,1280]{2,1,0:T(8,128)(2,1)} %bitcast.310), calls=%async_computation.12 | async-start | bytes 327680 | tf_op jit(solution)/shard_map/all_to_all | solution.py:27
  561.3 44.0 %all-reduce.14.cloned.1.call-start = ((), (), s32[]{:S(2)}) async-start(), calls=%async_computation.17 | async-start | bytes 196608 | tf_op jit(solution)/shard_map/psum | solution.py:133
  610.8 11.5 %all-to-all-start.13 = ((bf16[8,8,1280]{2,1,0:T(8,128)(2,1)}), bf16[8,8,1280]{2,1,0:T(8,128)(2,1)}, u32[]{:S(2)}, u32[]{:S(2)}) async-start(bf16[8,8,1280]{2,1,0:T(8,128)(2,1)} %fusion.76), calls=%async_computation.13 | async-start | bytes 327680 | tf_op jit(solution)/shard_map/all_to_all | solution.py:27
  626.3 32.2 %collective-permute-start.5 = (bf16[128,5120]{1,0:T(8,128)(2,1)S(1)}, bf16[128,5120]{1,0:T(8,128)(2,1)}, u32[]{:S(2)}, u32[]{:S(2)}) collective-permute-start(bf16[128,5120]{1,0:T(8,128)(2,1)S(1)} %fusion.47), channel_id=1, source_target_pairs={{2,0},{4,2},{6,4},{3,1},{5,3},{7,5},{10,8},{12,10},{14,12},{11,9},... | collective-permute-start | bytes 3932168 | tf_op jit(solution)/shard_map/ppermute | solution.py:12
  664.6 11.2 %all-to-all-start.14 = ((bf16[8,8,1280]{2,1,0:T(8,128)(2,1)}), bf16[8,8,1280]{2,1,0:T(8,128)(2,1)}, u32[]{:S(2)}, u32[]{:S(2)}) async-start(bf16[8,8,1280]{2,1,0:T(8,128)(2,1)} %bitcast.311), calls=%async_computation.14 | async-start | bytes 327680 | tf_op jit(solution)/shard_map/all_to_all | solution.py:27
  668.6 43.2 %all-reduce.16.cloned.1.call-start = ((), (), s32[]{:S(2)}) async-start(), calls=%async_computation.18 | async-start | bytes 196608 | tf_op jit(solution)/shard_map/psum | solution.py:133
  717.4 11.2 %all-to-all-start.15 = ((bf16[8,8,1280]{2,1,0:T(8,128)(2,1)}), bf16[8,8,1280]{2,1,0:T(8,128)(2,1)}, u32[]{:S(2)}, u32[]{:S(2)}) async-start(bf16[8,8,1280]{2,1,0:T(8,128)(2,1)} %fusion.75), calls=%async_computation.15 | async-start | bytes 327680 | tf_op jit(solution)/shard_map/all_to_all | solution.py:27
  (50 other events, 280.8 us)
Sparse Core Ops, SparseCore 0:
  35.2 34.2 all-reduce.23
  142.9 35.1 all-reduce.21
  250.7 35.1 all-reduce.19
  360.6 36.4 all-reduce.17
  466.2 33.9 all-reduce.11
  570.9 34.2 all-reduce.13
  678.3 33.4 all-reduce.15
where the time goes:
time: 753 us; the launch traced here: 742 us
  waiting for transfers between devices  399 us (53%)
  matrix products  105 us (14%)
  blocking collectives  87.3 us (12%)
  local copies, waits for them, and re-layouts  49.4 us (7%)
  starting transfers between devices  45.8 us (6%)
  other arithmetic  40.5 us (5%)
  between operations  15.4 us (2%)
    psum x4, waiting for transfers between devices, local(): lax.psum(up_part.astype(jnp.bfloat16), 'dp').astype(jnp.float32)  142 us
    ppermute x6, waiting for transfers between devices, from_behind(): lax.ppermute(value, axis, [(source, source + steps) for source in range(l...  136 us
    psum x3, waiting for transfers between devices, local(): lax.psum(hidden_part.astype(jnp.bfloat16), 'dp').astype(jnp.float32)  96.3 us
    all_to_all x8, blocking collectives, deliver(): lax.all_to_all(flat_buffer, ('dp', 'expert'), split_axis=0, concat_axis=0...  87.3 us
    all_to_all x8, starting transfers between devices, deliver(): lax.all_to_all(flat_buffer, ('dp', 'expert'), split_axis=0, concat_axis=0...  30.9 us
    all_to_all x8, waiting for transfers between devices, deliver(): lax.all_to_all(flat_buffer, ('dp', 'expert'), split_axis=0, concat_axis=0...  25.2 us
  transfers between devices with their start and end apart: 21, of which 20 were waited for; matrix products, arithmetic and copies ran while one was open for 8% of the time, Pallas kernels for 0%

commit v1 on v0

v1 whole, which is shorter than its diff:
```python
import functools

import jax
import jax.numpy as jnp
from jax import lax
from jax.experimental import pallas as pl
from jax.experimental.pallas import tpu as pltpu
from jax.sharding import PartitionSpec as P

CAP = 8
EPS = 1e-06
F32 = jnp.float32
BF16 = jnp.bfloat16
FIRST = (((0,), (0,)), ((), ()))
SECOND = (((1,), (1,)), ((), ()))


def split(value):
    high = value.astype(BF16)
    return high, (value - high.astype(F32)).astype(BF16)


def join(ref_value):
    wide = ref_value.astype(F32)
    return wide[:, :128] + wide[:, 128:]


def kernel(
    nz, nl, ne,
    tok_in, cot_in, gain, gates, ids, emap, wg_in, wu_in, wd_in,
    out_f, out_b, out_g, out_u, out_d,
    tok, cot, wg, wu, wd,
    d_send, d_recv, m_send, m_recv, idsall, cross, own_b, r_send, r_recv,
    a_ref, g_ref, part, part_in, act_all, hpart, hpart_in, grad_all,
    gp_ref, up_ref, inv_ref,
    load_sem, store_sem, d_ss, d_rs, m_ss, m_rs, i_ss, i_rs, c_ss, c_rs,
    f_ss, f_rs, x_ss, x_rs, r_ss, r_rs,
):
    z, s, p = lax.axis_index("dp"), lax.axis_index("section"), lax.axis_index("expert")
    nb = nz * ne
    me = z * ne + p
    rows = ne * CAP
    slots = nb * CAP
    toks, width = tok.shape
    dsl = width // nz
    half = dsl // 2
    hid = wg.shape[1]

    def rdma(src, dst, ss, rs, zz, sec, ex):
        return pltpu.make_async_remote_copy(
            src_ref=src, dst_ref=dst, send_sem=ss, recv_sem=rs,
            device_id={"dp": zz, "section": sec, "expert": ex},
            device_id_type=pl.DeviceIdType.MESH,
        )

    loads = [
        pltpu.make_async_copy(a, b, load_sem.at[i])
        for i, (a, b) in enumerate(
            ((tok_in, tok), (cot_in, cot), (wg_in, wg), (wu_in, wu), (wd_in, wd))
        )
    ]
    for copy in loads:
        copy.start()

    barrier = pltpu.get_barrier_semaphore()

    def greet(d, _):
        other = lax.rem(me + d, nb)
        pl.semaphore_signal(
            barrier, inc=1,
            device_id={"dp": other // ne, "section": s, "expert": lax.rem(other, ne)},
            device_id_type=pl.DeviceIdType.MESH,
        )
        return 0

    lax.fori_loop(1, nb, greet, 0)

    def greet_section(d, _):
        pl.semaphore_signal(
            barrier, inc=1,
            device_id={"dp": z, "section": lax.rem(s + d, nl), "expert": p},
            device_id_type=pl.DeviceIdType.MESH,
        )
        return 0

    lax.fori_loop(1, nl, greet_section, 0)

    lane = lax.broadcasted_iota(jnp.int32, (toks, 128), 1)
    row = lax.broadcasted_iota(jnp.int32, (toks, 128), 0)
    expert = jnp.full((toks, 128), -1, jnp.int32)
    place = lane
    for e in range(ne):
        here = (lane >= e * CAP) & (lane < (e + 1) * CAP)
        expert = jnp.where(here, emap[0, e], expert)
        place = jnp.where(here, lane - e * CAP, place)
    chosen = jnp.zeros((toks, 128), F32)
    weight = jnp.zeros((toks, 128), F32)
    for k in range(ids.shape[1]):
        match = ids[:, k : k + 1] == expert
        chosen = chosen + jnp.where(match, 1.0, 0.0)
        weight = weight + jnp.where(match, gates[:, k : k + 1], 0.0)
    tri_r = lax.broadcasted_iota(jnp.int32, (toks, toks), 0)
    tri_c = lax.broadcasted_iota(jnp.int32, (toks, toks), 1)
    tri = jnp.where(tri_r >= tri_c, 1.0, 0.0).astype(BF16)
    rank = jnp.dot(tri, chosen.astype(BF16), preferred_element_type=F32)
    placed = jnp.where(rank - 1.0 == place.astype(F32), chosen, 0.0)
    placed_t = jnp.transpose(placed)[:rows]
    r_col = jnp.sum(jnp.transpose(placed * weight)[:rows], axis=1, keepdims=True)
    t_col = jnp.sum(
        jnp.transpose(placed * (row + 1).astype(F32))[:rows], axis=1, keepdims=True
    )
    base = (me * toks).astype(F32)
    t_col = jnp.where(t_col > 0.5, t_col - 1.0 + base, -1.0)
    m_send[:, :128] = jnp.broadcast_to(r_col, (rows, 128))
    m_send[:, 128:] = jnp.broadcast_to(t_col, (rows, 128))
    m_recv[me] = m_send[...]
    pick = placed_t.astype(BF16)

    pl.semaphore_wait(barrier, nb - 1 + nl - 1)

    def pack(value):
        return jnp.concatenate([value[..., :half], value[..., half:]], axis=-2)

    def gather(kind, source):
        for q in range(nz):
            got = jnp.dot(
                pick, source[:, q * dsl : (q + 1) * dsl], preferred_element_type=F32
            )
            for e in range(ne):
                d_send[kind, q * ne + e] = pack(got[e * CAP : (e + 1) * CAP]).astype(BF16)
        d_recv[kind, me] = d_send[kind, me]

    def dispatch(kind):
        def send(d, _):
            other = lax.rem(me + d, nb)
            rdma(
                d_send.at[kind, other], d_recv.at[kind, me], d_ss.at[kind, d], d_rs.at[kind, d],
                other // ne, s, lax.rem(other, ne),
            ).start()
            return 0

        lax.fori_loop(1, nb, send, 0)

    def dispatch_wait(kind, sent):
        def wait(d, _):
            other = lax.rem(me + nb - d, nb)
            copy = rdma(
                d_send.at[kind, other], d_recv.at[kind, other], d_ss.at[kind, d],
                d_rs.at[kind, d], other // ne, s, lax.rem(other, ne),
            )
            if sent:
                copy.wait_send()
            else:
                copy.wait_recv()
            return 0

        lax.fori_loop(1, nb, wait, 0)

    def meta(action):
        def step(d, _):
            other = lax.rem(me + d, nb)
            source = lax.rem(me + nb - d, nb)
            where = me if action == "start" else source
            copy = rdma(
                m_send, m_recv.at[where], m_ss.at[d], m_rs.at[d],
                other // ne, s, lax.rem(other, ne),
            )
            getattr(copy, action)()
            return 0

        lax.fori_loop(1, nb, step, 0)

    def exchange_ids(action):
        def step(d, _):
            other = lax.rem(s + d, nl)
            source = lax.rem(s + nl - d, nl)
            where = s if action == "start" else source
            copy = rdma(idsall.at[s], idsall.at[where], i_ss.at[d], i_rs.at[d], z, other, p)
            getattr(copy, action)()
            return 0

        lax.fori_loop(1, nl, step, 0)

    meta("start")
    loads[0].wait()
    gather(0, tok)
    dispatch(0)
    loads[1].wait()
    gather(1, cot)
    dispatch(1)
    meta("wait_recv")
    idsall[s] = m_recv[:, :, 128:]
    exchange_ids("start")

    own_rows = pl.ds(pl.multiple_of(p * CAP, CAP), CAP)
    own_meta = m_recv[:, own_rows, :].reshape(slots, 256)
    r_slot = own_meta[:, 0:1]
    t_slot = own_meta[:, 128:129]
    gain_row = gain[:, pl.ds(pl.multiple_of(z * dsl, 128), dsl)]

    def unpack(kind):
        value = d_recv[kind].astype(F32)
        return jnp.concatenate([value[:, :CAP], value[:, CAP:]], axis=-1).reshape(slots, dsl)

    dispatch_wait(0, False)
    a_ref[...] = unpack(0)

    def over_dp(action, send_at, recv_at, which):
        def step(d, _):
            other = lax.rem(z + d, nz)
            source = lax.rem(z + nz - d, nz)
            where = z if action == "start" else source
            copy = rdma(
                send_at(other), recv_at(where), c_ss.at[which, d], c_rs.at[which, d],
                other, s, p,
            )
            getattr(copy, action)()
            return 0

        lax.fori_loop(1, nz, step, 0)

    def block(ref):
        return lambda other: ref.at[pl.ds(pl.multiple_of(other * rows, 16), rows)]

    def mine(ref):
        return lambda other: ref.at[z]

    def at(ref):
        return lambda where: ref.at[where]

    def return_rows(kind, layer, value):
        r_send[kind, layer] = pack(value.reshape(nb, CAP, dsl)).astype(BF16)
        r_recv[kind, layer, me] = r_send[kind, layer, me]

        def send(d, _):
            other = lax.rem(me + d, nb)
            rdma(
                r_send.at[kind, layer, other], r_recv.at[kind, layer, me],
                r_ss.at[kind, layer, d], r_rs.at[kind, layer, d],
                other // ne, s, lax.rem(other, ne),
            ).start()
            return 0

        lax.fori_loop(1, nb, send, 0)

    def return_wait(kind, layer, sent):
        def wait(d, _):
            other = lax.rem(me + nb - d, nb)
            copy = rdma(
                r_send.at[kind, layer, other], r_recv.at[kind, layer, other],
                r_ss.at[kind, layer, d], r_rs.at[kind, layer, d],
                other // ne, s, lax.rem(other, ne),
            )
            if sent:
                copy.wait_send()
            else:
                copy.wait_recv()
            return 0

        lax.fori_loop(1, nb, wait, 0)

    def to_section(kind, layer, src, sec):
        return rdma(
            src, cross.at[layer, p], f_ss.at[kind, layer], f_rs.at[kind, layer], z, sec, p
        )

    def share(layer, action):
        def step(d, _):
            other = lax.rem(p + d, ne)
            source = lax.rem(p + ne - d, ne)
            where = p if action != "wait_recv" else source
            copy = rdma(
                cross.at[layer, p], cross.at[layer, where], x_ss.at[layer, d],
                x_rs.at[layer, d], z, s, other,
            )
            getattr(copy, action)()
            return 0

        lax.fori_loop(1, ne, step, 0)

    def receive(kind, layer, state, step_to, last):
        matches = []
        for e in range(ne):
            theirs = idsall[layer, :, e * CAP : (e + 1) * CAP, :].reshape(slots, 128)
            theirs = jnp.transpose(theirs)[0:1]
            matches.append(jnp.where(t_slot == theirs, 1.0, 0.0).astype(BF16))
        to_section(kind, layer, cross.at[layer, p], lax.rem(s + nl + step_to, nl)).wait_recv()
        share(layer, "start")

        @pl.when(s != last)
        def _():
            to_section(kind, layer, cross.at[layer, p], lax.rem(s + nl + step_to, nl)).start()

        share(layer, "wait_recv")
        total = state[...]
        for e in range(ne):
            total = total + jnp.dot(matches[e], cross[layer, e], preferred_element_type=F32)
        state[...] = total.astype(BF16).astype(F32)
        return_rows(kind, layer, cross[layer, p].astype(F32))

    exchange_ids("wait_recv")

    def forward_receive(layer, _):
        receive(0, layer, a_ref, 1, nl - 1)
        return 0

    lax.fori_loop(0, s, forward_receive, 0)

    wide = a_ref[...]
    x = (wide * gain_row).astype(BF16)
    square = jnp.sum(wide * wide, axis=1, keepdims=True)
    loads[2].wait()
    part[:, :hid] = jnp.dot(x, wg[...], preferred_element_type=F32).astype(BF16)
    loads[3].wait()
    part[:, hid : 2 * hid] = jnp.dot(x, wu[...], preferred_element_type=F32).astype(BF16)
    high, low = split(jnp.broadcast_to(square, (slots, 128)))
    part[:, 2 * hid : 2 * hid + 128] = high
    part[:, 2 * hid + 128 :] = low
    over_dp("start", block(part), at(part_in), 0)
    part_in[z] = part[pl.ds(pl.multiple_of(z * rows, 16), rows)]
    over_dp("wait_recv", block(part), at(part_in), 0)
    total = part_in[0].astype(F32)
    for i in range(1, nz):
        total = total + part_in[i].astype(F32)
    inv = lax.rsqrt(join(total[:, 2 * hid :])[:, :1] / width + EPS)
    gate_pre = total[:, :hid] * inv
    up_pre = total[:, hid : 2 * hid] * inv
    gp_ref[...] = gate_pre
    up_ref[...] = up_pre
    inv_ref[...] = jnp.broadcast_to(inv, (rows, 128))
    act_all[z, :, :hid] = (gate_pre * jax.nn.sigmoid(gate_pre) * up_pre).astype(BF16)
    high, low = split(inv_ref[...])
    act_all[z, :, hid : hid + 128] = high
    act_all[z, :, hid + 128 :] = low
    over_dp("start", mine(act_all), at(act_all), 1)
    loads[4].wait()
    over_dp("wait_recv", mine(act_all), at(act_all), 1)
    act = act_all[...].reshape(slots, hid + 256)
    out_rows = r_slot * jnp.dot(act[:, :hid], wd[...], preferred_element_type=F32)
    cross[s, p] = out_rows.astype(BF16)

    @pl.when(s != nl - 1)
    def _():
        to_section(0, s, cross.at[s, p], lax.rem(s + 1, nl)).start()

    return_rows(0, s, cross[s, p].astype(F32))
    dispatch_wait(1, False)
    g_ref[...] = unpack(1)

    def place_rows(kind, layer, acc):
        return_wait(kind, layer, False)
        want = lax.broadcasted_iota(jnp.int32, (rows, toks), 1).astype(F32) + base
        hot = jnp.where(idsall[layer, me][:, :1] == want, 1.0, 0.0).astype(BF16)
        for q in range(nz):
            got = r_recv[kind, layer, q * ne : (q + 1) * ne].astype(F32)
            got = jnp.concatenate([got[:, :CAP], got[:, CAP:]], axis=-1)
            got = got.reshape(rows, dsl).astype(BF16)
            add = lax.dot_general(hot, got, FIRST, preferred_element_type=F32)
            columns = slice(q * dsl, (q + 1) * dsl)
            acc[:, columns] = (acc[:, columns].astype(F32) + add).astype(BF16)

    store_f = pltpu.make_async_copy(tok, out_f, store_sem.at[0])

    def finish_forward():
        def step(layer, _):
            place_rows(0, layer, tok)
            return 0

        lax.fori_loop(0, s + 1, step, 0)
        store_f.start()

    pl.when(s != nl - 1)(finish_forward)

    def backward_receive(i, _):
        receive(1, nl - 1 - i, g_ref, -1, 0)
        return 0

    lax.fori_loop(0, nl - 1 - s, backward_receive, 0)

    slot_grad = (r_slot * g_ref[...]).astype(BF16)
    hpart[...] = lax.dot_general(
        slot_grad, wd[...], SECOND, preferred_element_type=F32
    ).astype(BF16)
    over_dp("start", block(hpart), at(hpart_in), 2)
    hpart_in[z] = hpart[pl.ds(pl.multiple_of(z * rows, 16), rows)]
    gate_pre = gp_ref[...]
    up_pre = up_ref[...]
    sig = jax.nn.sigmoid(gate_pre)
    over_dp("wait_recv", block(hpart), at(hpart_in), 2)
    hidden = hpart_in[0].astype(F32)
    for i in range(1, nz):
        hidden = hidden + hpart_in[i].astype(F32)
    gate_grad = (hidden * up_pre * sig * (1.0 + gate_pre * (1.0 - sig))).astype(BF16)
    up_grad = (hidden * gate_pre * sig).astype(BF16)
    grad_all[z, :, :hid] = gate_grad
    grad_all[z, :, hid : 2 * hid] = up_grad
    along = jnp.sum(
        gate_grad.astype(F32) * gate_pre + up_grad.astype(F32) * up_pre, axis=1, keepdims=True
    )
    inv = inv_ref[...]
    high, low = split(inv * inv * along / width)
    grad_all[z, :, 2 * hid : 2 * hid + 128] = high
    grad_all[z, :, 2 * hid + 128 :] = low
    over_dp("start", mine(grad_all), at(grad_all), 3)
    over_dp("wait_recv", mine(grad_all), at(grad_all), 3)
    grads = grad_all[...].reshape(slots, 2 * hid + 256)
    act = act_all[...].reshape(slots, hid + 256)
    inv_slot = join(act[:, hid:])[:, :1]
    factor = join(grads[:, 2 * hid :])[:, :1]
    back = lax.dot_general(
        grads[:, :hid], wg[...], SECOND, preferred_element_type=F32
    ) + lax.dot_general(grads[:, hid : 2 * hid], wu[...], SECOND, preferred_element_type=F32)
    own_b[...] = (inv_slot * (gain_row * back) - a_ref[...] * factor).astype(BF16)

    @pl.when(s != 0)
    def _():
        to_section(1, s, own_b, lax.rem(s + nl - 1, nl)).start()

    return_rows(1, s, own_b[...].astype(F32))

    normed = (a_ref[...] * inv_slot * gain_row).astype(BF16)
    step_w = 256 if dsl % 256 == 0 else 128
    stores = []
    for start in range(0, dsl, step_w):
        left = normed[:, start : start + step_w]
        for out, lo in ((wg, 0), (wu, hid)):
            out[start : start + step_w, :] = lax.dot_general(
                left, grads[:, lo : lo + hid], FIRST, preferred_element_type=F32
            ).astype(BF16)
    stores.append(pltpu.make_async_copy(wg, out_g, store_sem.at[2]))
    stores.append(pltpu.make_async_copy(wu, out_u, store_sem.at[3]))
    stores[0].start()
    stores[1].start()
    step_h = 256 if hid % 256 == 0 else 128
    slot_grad = (r_slot * g_ref[...]).astype(BF16)
    for start in range(0, hid, step_h):
        wd[start : start + step_h, :] = lax.dot_general(
            act[:, start : start + step_h], slot_grad, FIRST, preferred_element_type=F32
        ).astype(BF16)
    stores.append(pltpu.make_async_copy(wd, out_d, store_sem.at[4]))
    stores[2].start()

    pl.when(s == nl - 1)(finish_forward)

    def finish_backward(i, _):
        place_rows(1, nl - 1 - i, cot)
        return 0

    lax.fori_loop(0, nl - s, finish_backward, 0)
    store_b = pltpu.make_async_copy(cot, out_b, store_sem.at[1])
    store_b.start()

    dispatch_wait(0, True)
    dispatch_wait(1, True)
    meta("wait_send")
    exchange_ids("wait_send")
    over_dp("wait_send", block(part), at(part_in), 0)
    over_dp("wait_send", mine(act_all), at(act_all), 1)
    over_dp("wait_send", block(hpart), at(hpart_in), 2)
    over_dp("wait_send", mine(grad_all), at(grad_all), 3)

    def drain_forward(layer, _):
        return_wait(0, layer, True)

        @pl.when(s != nl - 1)
        def _():
            to_section(0, layer, cross.at[layer, p], lax.rem(s + 1, nl)).wait_send()

        return 0

    lax.fori_loop(0, s + 1, drain_forward, 0)

    def drain_backward(layer, _):
        return_wait(1, layer, True)

        @pl.when((s != 0) & (layer != s))
        def _():
            to_section(1, layer, cross.at[layer, p], lax.rem(s + nl - 1, nl)).wait_send()

        return 0

    lax.fori_loop(s, nl, drain_backward, 0)

    @pl.when(s != 0)
    def _():
        to_section(1, s, own_b, lax.rem(s + nl - 1, nl)).wait_send()

    def drain_share(layer, _):
        share(layer, "wait_send")
        return 0

    lax.fori_loop(0, s, drain_share, 0)
    lax.fori_loop(s + 1, nl, drain_share, 0)
    for copy in stores:
        copy.wait()
    store_f.wait()
    store_b.wait()


def local(
    tokens, cotangent, norm_gain, route_gates, expert_ids, expert_map, w_gate, w_up, w_down
):
    nz, nl, ne = (lax.axis_size(n) for n in ("dp", "section", "expert"))
    toks, width = tokens.shape
    dsl, hid = w_gate.shape[2:]
    nb = nz * ne
    rows = ne * CAP
    slots = nb * CAP
    half = dsl // 2
    vm = pltpu.VMEM
    dma = pltpu.SemaphoreType.DMA
    anywhere = pl.BlockSpec(memory_space=pl.ANY)
    vmem = pl.BlockSpec(memory_space=pltpu.VMEM)
    smem = pl.BlockSpec(memory_space=pltpu.SMEM)
    out = functools.partial(jax.ShapeDtypeStruct, dtype=BF16)
    results = pl.pallas_call(
        functools.partial(kernel, nz, nl, ne),
        out_shape=(
            out((toks, width)), out((toks, width)), out((dsl, hid)), out((dsl, hid)),
            out((hid, dsl)),
        ),
        in_specs=[anywhere, anywhere, vmem, vmem, vmem, smem, anywhere, anywhere, anywhere],
        out_specs=(anywhere,) * 5,
        scratch_shapes=[
            vm((toks, width), BF16), vm((toks, width), BF16),
            vm((dsl, hid), BF16), vm((dsl, hid), BF16), vm((hid, dsl), BF16),
            vm((2, nb, 2 * CAP, half), BF16), vm((2, nb, 2 * CAP, half), BF16),
            vm((rows, 256), F32), vm((nb, rows, 256), F32),
            vm((nl, nb, rows, 128), F32),
            vm((nl, ne, slots, dsl), BF16), vm((slots, dsl), BF16),
            vm((2, nl, nb, 2 * CAP, half), BF16), vm((2, nl, nb, 2 * CAP, half), BF16),
            vm((slots, dsl), F32), vm((slots, dsl), F32),
            vm((slots, 2 * hid + 256), BF16), vm((nz, rows, 2 * hid + 256), BF16),
            vm((nz, rows, hid + 256), BF16),
            vm((slots, hid), BF16), vm((nz, rows, hid), BF16),
            vm((nz, rows, 2 * hid + 256), BF16),
            vm((rows, hid), F32), vm((rows, hid), F32), vm((rows, 128), F32),
            dma((5,)), dma((5,)),
            dma((2, nb)), dma((2, nb)), dma((nb,)), dma((nb,)),
            dma((nl,)), dma((nl,)), dma((4, nz)), dma((4, nz)),
            dma((2, nl)), dma((2, nl)), dma((nl, ne)), dma((nl, ne)),
            dma((2, nl, nb)), dma((2, nl, nb)),
        ],
        compiler_params=pltpu.CompilerParams(
            collective_id=0, has_side_effects=True, vmem_limit_bytes=58 * 2**20
        ),
    )(
        tokens, cotangent, norm_gain, route_gates[0], expert_ids[0], expert_map,
        w_gate[0, 0], w_up[0, 0], w_down[0, 0],
    )
    layer_out, input_grad, gate, up, down = results
    return layer_out[None], input_grad[None], gate[None, None], up[None, None], down[None, None]


def solution(mesh):
    tokens = P(("dp", "expert"), None)
    routed = P("section", ("dp", "expert"), None)
    wide = P("section", "expert", "dp", None)
    tall = P("section", "expert", None, "dp")
    return jax.shard_map(
        local,
        mesh=mesh,
        in_specs=(
            tokens, tokens, P("section", None), routed, routed, P("section", None),
            wide, wide, tall,
        ),
        out_specs=(routed, routed, wide, wide, tall),
        check_vma=False,
    )
```

time: 753 us -> 194 us (0.26); the launches traced: 742 us -> 194 us
  waiting for transfers between devices: 399 us -> 0 us
  Pallas kernels: 0 us -> 180 us
  matrix products: 105 us -> 0 us
  blocking collectives: 87.3 us -> 0 us
  starting transfers between devices: 45.8 us -> 0 us
  other arithmetic: 40.5 us -> 0 us
  local copies, waits for them, and re-layouts: 49.4 us -> 13.2 us
  between operations: 15.4 us -> 0.65 us
    psum x7 -> x0, waiting for transfers between devices: 238 us -> none  [the longest x4 142 us: local(): lax.psum(up_part.astype(jnp.bfloat16), 'dp').astype(jnp.float32)]
    pallas_call x0 -> x1, Pallas kernels: none -> 180 us  [local(): pl.pallas_call(functools.partial(kernel, nz, nl, ne), out_shape=(out((tok...]
    ppermute x6 -> x0, waiting for transfers between devices: 136 us -> none  [from_behind(): lax.ppermute(value, axis, [(source, source + steps) for source in range(l...]
    dot_general x52 -> x0, matrix products: 105 us -> none  [the longest x4 11.8 us: local(): lax.dot_general(slot_rows, gate_grad, contract_first, preferred_element_t...]
    all_to_all x8 -> x0, blocking collectives: 87.3 us -> none  [deliver(): lax.all_to_all(flat_buffer, ('dp', 'expert'), split_axis=0, concat_axis=0...]
    all_to_all x8 -> x0, starting transfers between devices: 30.9 us -> none  [deliver(): lax.all_to_all(flat_buffer, ('dp', 'expert'), split_axis=0, concat_axis=0...]
    reshape x12 -> x0, local copies, waits for them, and re-layouts: 29.7 us -> none  [the longest x4 14.8 us: local(): normed.reshape(forward_rows_here, dp_groups, slice_width)]
    convert_element_type x15 -> x0, other arithmetic: 25.8 us -> none  [the longest x3 7.05 us: local(): result = (forward_wide_in + combined).astype(jnp.bfloat16)]
  transfers between devices with their start and end apart: 21 -> 0, of which waited for: 20 -> 0; matrix products, arithmetic and copies ran while one was open for 8% -> 0% of each run, Pallas kernels for 0% -> 0%
where the time goes in v1:
time: 194 us
  Pallas kernels  180 us (93%)
  local copies, waits for them, and re-layouts  13.2 us (7%)
    pallas_call x1, Pallas kernels, local(): pl.pallas_call(functools.partial(kernel, nz, nl, ne), out_shape=(out((tok...  180 us
    unnamed x15, local copies, waits for them, and re-layouts  13.2 us

profile of v1, /device:TPU:0, one launch (start us, length us, event | category | flops | bytes accessed | tf_op | source)
XLA Modules:
  0.0 193.8 jit_solution(4597875622053652069)
XLA Ops:
  0.6 1.4 copy.14
  2.1 1.4 copy.15
  3.5 179.9 %shard_map.128 = (bf16[128,5120]{1,0:T(8,128)(2,1)}, bf16[128,5120]{1,0:T(8,128)(2,1)}, bf16[1280,768]{1,0:T(8,128)(2,1)}, bf16[1280,768]{1,0:T(8,128)(2,1)}, bf16[768,1280]{1,0:T(8,128)(2,1)}) custom-call(bf16[128,5120]{1,0:T(8,128)(2,1)} %tok_in.1, bf16[128,5120]{1,0:T(8,128)(2,1)} %cot_in.1, f32[1,5120]{1,0:T(1,128)} %gain.1, f32[128,6]{1,0:T(8,128)} %bitcast.18, ...), custom_call_target="tpu_custom_call" | custom-call | tf_op jit(solution)/shard_map/pallas_call | solution.py:516
  183.4 0.0 copy-start.3
  183.4 2.6 %copy.21 = bf16[1,128,5120]{2,1,0:T(8,128)(2,1)} copy(bf16[1,128,5120]{2,1,0:T(8,128)(2,1)} %bitcast.17) | data formatting | bytes 2621440
  186.0 0.0 copy-done.3
  186.0 0.0 copy-start.2
  186.0 1.1 copy.22
  187.0 1.0 copy-done.2
  188.0 0.0 copy-start.1
  188.0 1.3 copy.23
  189.3 1.0 copy-done.1
  190.2 0.0 copy-start
  190.2 1.3 copy.24
  191.5 1.0 copy-done
  192.5 1.3 copy.25
Async XLA Ops:
  183.4 2.6 %copy-start.3 = (bf16[128,5120]{1,0:T(8,128)(2,1)S(1)}, bf16[128,5120]{1,0:T(8,128)(2,1)}, u32[]{:S(2)}) copy-start(bf16[128,5120]{1,0:T(8,128)(2,1)} %get-tuple-element.11) | copy-start | bytes 3932164
  186.0 2.0 %copy-start.2 = (bf16[1280,768]{1,0:T(8,128)(2,1)S(1)}, bf16[1280,768]{1,0:T(8,128)(2,1)}, u32[]{:S(2)}) copy-start(bf16[1280,768]{1,0:T(8,128)(2,1)} %get-tuple-element.12) | copy-start | bytes 5898244
  188.0 2.3 %copy-start.1 = (bf16[1280,768]{1,0:T(8,128)(2,1)S(1)}, bf16[1280,768]{1,0:T(8,128)(2,1)}, u32[]{:S(2)}) copy-start(bf16[1280,768]{1,0:T(8,128)(2,1)} %get-tuple-element.13) | copy-start | bytes 5898244
  190.2 2.3 %copy-start = (bf16[768,1280]{1,0:T(8,128)(2,1)S(1)}, bf16[768,1280]{1,0:T(8,128)(2,1)}, u32[]{:S(2)}) copy-start(bf16[768,1280]{1,0:T(8,128)(2,1)} %get-tuple-element.14) | copy-start | bytes 5898244

commit v2 on v1

--- a/solution.py
+++ b/solution.py
@@ -8,6 +8,7 @@
 from jax.sharding import PartitionSpec as P
 
 CAP = 8
+TID = 64
 EPS = 1e-06
 F32 = jnp.float32
 BF16 = jnp.bfloat16
@@ -28,12 +29,11 @@
 def kernel(
     nz, nl, ne,
     tok_in, cot_in, gain, gates, ids, emap, wg_in, wu_in, wd_in,
-    out_f, out_b, out_g, out_u, out_d,
     tok, cot, wg, wu, wd,
-    d_send, d_recv, m_send, m_recv, idsall, cross, own_b, r_send, r_recv,
+    d_send, d_recv, m_send, idsall, cross, own_b, r_send, r_recv,
     a_ref, g_ref, part, part_in, act_all, hpart, hpart_in, grad_all,
     gp_ref, up_ref, inv_ref,
-    load_sem, store_sem, d_ss, d_rs, m_ss, m_rs, i_ss, i_rs, c_ss, c_rs,
+    load_sem, d_ss, d_rs, m_ss, m_rs, i_ss, i_rs, c_ss, c_rs,
     f_ss, f_rs, x_ss, x_rs, r_ss, r_rs,
 ):
     z, s, p = lax.axis_index("dp"), lax.axis_index("section"), lax.axis_index("expert")
@@ -85,36 +85,33 @@
 
     lax.fori_loop(1, nl, greet_section, 0)
 
-    lane = lax.broadcasted_iota(jnp.int32, (toks, 128), 1)
-    row = lax.broadcasted_iota(jnp.int32, (toks, 128), 0)
-    expert = jnp.full((toks, 128), -1, jnp.int32)
-    place = lane
+    row = lax.broadcasted_iota(jnp.int32, (rows, toks), 0)
+    token = lax.broadcasted_iota(jnp.int32, (rows, toks), 1)
+    expert = jnp.full((rows, toks), -1, jnp.int32)
+    place = row
     for e in range(ne):
-        here = (lane >= e * CAP) & (lane < (e + 1) * CAP)
+        here = (row >= e * CAP) & (row < (e + 1) * CAP)
         expert = jnp.where(here, emap[0, e], expert)
-        place = jnp.where(here, lane - e * CAP, place)
-    chosen = jnp.zeros((toks, 128), F32)
-    weight = jnp.zeros((toks, 128), F32)
-    for k in range(ids.shape[1]):
-        match = ids[:, k : k + 1] == expert
+        place = jnp.where(here, row - e * CAP, place)
+    chosen = jnp.zeros((rows, toks), F32)
+    weight = jnp.zeros((rows, toks), F32)
+    for k in range(ids.shape[0]):
+        match = ids[k] == expert
         chosen = chosen + jnp.where(match, 1.0, 0.0)
-        weight = weight + jnp.where(match, gates[:, k : k + 1], 0.0)
+        weight = weight + jnp.where(match, gates[k], 0.0)
     tri_r = lax.broadcasted_iota(jnp.int32, (toks, toks), 0)
     tri_c = lax.broadcasted_iota(jnp.int32, (toks, toks), 1)
-    tri = jnp.where(tri_r >= tri_c, 1.0, 0.0).astype(BF16)
-    rank = jnp.dot(tri, chosen.astype(BF16), preferred_element_type=F32)
+    tri = jnp.where(tri_r <= tri_c, 1.0, 0.0).astype(BF16)
+    rank = jnp.dot(chosen.astype(BF16), tri, preferred_element_type=F32)
     placed = jnp.where(rank - 1.0 == place.astype(F32), chosen, 0.0)
-    placed_t = jnp.transpose(placed)[:rows]
-    r_col = jnp.sum(jnp.transpose(placed * weight)[:rows], axis=1, keepdims=True)
-    t_col = jnp.sum(
-        jnp.transpose(placed * (row + 1).astype(F32))[:rows], axis=1, keepdims=True
-    )
+    r_col = jnp.sum(placed * weight, axis=1, keepdims=True)
+    t_col = jnp.sum(placed * (token + 1).astype(F32), axis=1, keepdims=True)
     base = (me * toks).astype(F32)
     t_col = jnp.where(t_col > 0.5, t_col - 1.0 + base, -1.0)
-    m_send[:, :128] = jnp.broadcast_to(r_col, (rows, 128))
-    m_send[:, 128:] = jnp.broadcast_to(t_col, (rows, 128))
-    m_recv[me] = m_send[...]
-    pick = placed_t.astype(BF16)
+    lane = lax.broadcasted_iota(jnp.int32, (rows, 128), 1)
+    m_send[...] = jnp.where(lane < TID, r_col, t_col)
+    idsall[s, me] = m_send[...]
+    pick = placed.astype(BF16)
 
     pl.semaphore_wait(barrier, nb - 1 + nl - 1)
 
@@ -162,7 +159,7 @@
             source = lax.rem(me + nb - d, nb)
             where = me if action == "start" else source
             copy = rdma(
-                m_send, m_recv.at[where], m_ss.at[d], m_rs.at[d],
+                m_send, idsall.at[s, where], m_ss.at[d], m_rs.at[d],
                 other // ne, s, lax.rem(other, ne),
             )
             getattr(copy, action)()
@@ -181,21 +178,30 @@
 
         lax.fori_loop(1, nl, step, 0)
 
-    meta("start")
     loads[0].wait()
     gather(0, tok)
     dispatch(0)
-    loads[1].wait()
-    gather(1, cot)
-    dispatch(1)
-    meta("wait_recv")
-    idsall[s] = m_recv[:, :, 128:]
-    exchange_ids("start")
+    meta("start")
+
+    def meta_settle():
+        meta("wait_recv")
+        exchange_ids("start")
+
+    def cot_settle():
+        loads[1].wait()
+        gather(1, cot)
+        dispatch(1)
+
+    @pl.when(s != 0)
+    def _():
+        meta_settle()
+        cot_settle()
 
     own_rows = pl.ds(pl.multiple_of(p * CAP, CAP), CAP)
-    own_meta = m_recv[:, own_rows, :].reshape(slots, 256)
-    r_slot = own_meta[:, 0:1]
-    t_slot = own_meta[:, 128:129]
+
+    def own_meta():
+        return idsall[s, :, own_rows, :].reshape(slots, 128)
+
     gain_row = gain[:, pl.ds(pl.multiple_of(z * dsl, 128), dsl)]
 
     def unpack(kind):
@@ -228,8 +234,9 @@
     def at(ref):
         return lambda where: ref.at[where]
 
-    def return_rows(kind, layer, value):
-        r_send[kind, layer] = pack(value.reshape(nb, CAP, dsl)).astype(BF16)
+    def return_rows(kind, layer, source):
+        value = source[...].astype(F32).reshape(2, nb, CAP, half)
+        r_send[kind, layer] = jnp.concatenate([value[0], value[1]], axis=1).astype(BF16)
         r_recv[kind, layer, me] = r_send[kind, layer, me]
 
         def send(d, _):
@@ -259,19 +266,20 @@
 
         lax.fori_loop(1, nb, wait, 0)
 
-    def to_section(kind, layer, src, sec):
+    def to_section(kind, layer, src, sec, c):
         return rdma(
-            src, cross.at[layer, p], f_ss.at[kind, layer], f_rs.at[kind, layer], z, sec, p
+            src, cross.at[layer, p, c], f_ss.at[kind, layer, c], f_rs.at[kind, layer, c],
+            z, sec, p,
         )
 
-    def share(layer, action):
+    def share(layer, action, c):
         def step(d, _):
             other = lax.rem(p + d, ne)
             source = lax.rem(p + ne - d, ne)
             where = p if action != "wait_recv" else source
             copy = rdma(
-                cross.at[layer, p], cross.at[layer, where], x_ss.at[layer, d],
-                x_rs.at[layer, d], z, s, other,
+                cross.at[layer, p, c], cross.at[layer, where, c], x_ss.at[layer, d, c],
+                x_rs.at[layer, d, c], z, s, other,
             )
             getattr(copy, action)()
             return 0
@@ -280,25 +288,48 @@
 
     def receive(kind, layer, state, step_to, last):
         matches = []
+        mine_t = own_meta()[:, TID : TID + 1]
         for e in range(ne):
             theirs = idsall[layer, :, e * CAP : (e + 1) * CAP, :].reshape(slots, 128)
-            theirs = jnp.transpose(theirs)[0:1]
-            matches.append(jnp.where(t_slot == theirs, 1.0, 0.0).astype(BF16))
-        to_section(kind, layer, cross.at[layer, p], lax.rem(s + nl + step_to, nl)).wait_recv()
-        share(layer, "start")
-
-        @pl.when(s != last)
-        def _():
-            to_section(kind, layer, cross.at[layer, p], lax.rem(s + nl + step_to, nl)).start()
-
-        share(layer, "wait_recv")
-        total = state[...]
-        for e in range(ne):
-            total = total + jnp.dot(matches[e], cross[layer, e], preferred_element_type=F32)
-        state[...] = total.astype(BF16).astype(F32)
-        return_rows(kind, layer, cross[layer, p].astype(F32))
-
-    exchange_ids("wait_recv")
+            theirs = jnp.transpose(theirs)[TID : TID + 1]
+            matches.append(jnp.where(mine_t == theirs, 1.0, 0.0).astype(BF16))
+        further = lax.rem(s + nl + step_to, nl)
+        for c in range(2):
+            to_section(kind, layer, cross.at[layer, p, c], further, c).wait_recv()
+            share(layer, "start", c)
+
+            @pl.when(s != last)
+            def _():
+                to_section(kind, layer, cross.at[layer, p, c], further, c).start()
+
+        for c in range(2):
+            share(layer, "wait_recv", c)
+            columns = slice(c * half, (c + 1) * half)
+            total = state[:, columns]
+            for e in range(ne):
+                total = total + jnp.dot(
+                    matches[e], cross[layer, e, c], preferred_element_type=F32
+                )
+            state[:, columns] = total.astype(BF16).astype(F32)
+
+    def part_back():
+        slot_grad = (own_meta()[:, 0:1] * g_ref[...]).astype(BF16)
+        hpart[...] = lax.dot_general(
+            slot_grad, wd[...], SECOND, preferred_element_type=F32
+        ).astype(BF16)
+        over_dp("start", block(hpart), at(hpart_in), 2)
+        hpart_in[z] = hpart[pl.ds(pl.multiple_of(z * rows, 16), rows)]
+
+    @pl.when(s != 0)
+    def _():
+        exchange_ids("wait_recv")
+
+    @pl.when(s == nl - 1)
+    def _():
+        dispatch_wait(1, False)
+        g_ref[...] = unpack(1)
+        loads[4].wait()
+        part_back()
 
     def forward_receive(layer, _):
         receive(0, layer, a_ref, 1, nl - 1)
@@ -318,6 +349,7 @@
     part[:, 2 * hid + 128 :] = low
     over_dp("start", block(part), at(part_in), 0)
     part_in[z] = part[pl.ds(pl.multiple_of(z * rows, 16), rows)]
+    pl.when(s == 0)(meta_settle)
     over_dp("wait_recv", block(part), at(part_in), 0)
     total = part_in[0].astype(F32)
     for i in range(1, nz):
@@ -333,24 +365,49 @@
     act_all[z, :, hid : hid + 128] = high
     act_all[z, :, hid + 128 :] = low
     over_dp("start", mine(act_all), at(act_all), 1)
-    loads[4].wait()
+
+    @pl.when(s == 0)
+    def _():
+        cot_settle()
+
+    @pl.when(s != nl - 1)
+    def _():
+        loads[4].wait()
+
+    r_slot = own_meta()[:, 0:1]
     over_dp("wait_recv", mine(act_all), at(act_all), 1)
     act = act_all[...].reshape(slots, hid + 256)
-    out_rows = r_slot * jnp.dot(act[:, :hid], wd[...], preferred_element_type=F32)
-    cross[s, p] = out_rows.astype(BF16)
+    for c in range(2):
+        out_rows = r_slot * jnp.dot(
+            act[:, :hid], wd[:, c * half : (c + 1) * half], preferred_element_type=F32
+        )
+        cross[s, p, c] = out_rows.astype(BF16)
+
+        @pl.when(s != nl - 1)
+        def _():
+            to_section(0, s, cross.at[s, p, c], lax.rem(s + 1, nl), c).start()
+
+    def return_forward():
+        def step(layer, _):
+            return_rows(0, layer, cross.at[layer, p])
+            return 0
+
+        lax.fori_loop(0, s + 1, step, 0)
 
     @pl.when(s != nl - 1)
     def _():
-        to_section(0, s, cross.at[s, p], lax.rem(s + 1, nl)).start()
-
-    return_rows(0, s, cross[s, p].astype(F32))
-    dispatch_wait(1, False)
-    g_ref[...] = unpack(1)
+        return_forward()
+        dispatch_wait(1, False)
+        g_ref[...] = unpack(1)
+
+    @pl.when(s == 0)
+    def _():
+        exchange_ids("wait_recv")
 
     def place_rows(kind, layer, acc):
         return_wait(kind, layer, False)
         want = lax.broadcasted_iota(jnp.int32, (rows, toks), 1).astype(F32) + base
-        hot = jnp.where(idsall[layer, me][:, :1] == want, 1.0, 0.0).astype(BF16)
+        hot = jnp.where(idsall[layer, me][:, TID : TID + 1] == want, 1.0, 0.0).astype(BF16)
         for q in range(nz):
             got = r_recv[kind, layer, q * ne : (q + 1) * ne].astype(F32)
             got = jnp.concatenate([got[:, :CAP], got[:, CAP:]], axis=-1)
@@ -359,30 +416,27 @@
             columns = slice(q * dsl, (q + 1) * dsl)
             acc[:, columns] = (acc[:, columns].astype(F32) + add).astype(BF16)
 
-    store_f = pltpu.make_async_copy(tok, out_f, store_sem.at[0])
-
     def finish_forward():
         def step(layer, _):
             place_rows(0, layer, tok)
             return 0
 
         lax.fori_loop(0, s + 1, step, 0)
-        store_f.start()
 
     pl.when(s != nl - 1)(finish_forward)
 
     def backward_receive(i, _):
         receive(1, nl - 1 - i, g_ref, -1, 0)
+
+        @pl.when(nl - 1 - i > s + 1)
+        def _():
+            return_rows(1, nl - 1 - i, cross.at[nl - 1 - i, p])
+
         return 0
 
     lax.fori_loop(0, nl - 1 - s, backward_receive, 0)
 
-    slot_grad = (r_slot * g_ref[...]).astype(BF16)
-    hpart[...] = lax.dot_general(
-        slot_grad, wd[...], SECOND, preferred_element_type=F32
-    ).astype(BF16)
-    over_dp("start", block(hpart), at(hpart_in), 2)
-    hpart_in[z] = hpart[pl.ds(pl.multiple_of(z * rows, 16), rows)]
+    pl.when(s != nl - 1)(part_back)
     gate_pre = gp_ref[...]
     up_pre = up_ref[...]
     sig = jax.nn.sigmoid(gate_pre)
@@ -402,43 +456,48 @@
     grad_all[z, :, 2 * hid : 2 * hid + 128] = high
     grad_all[z, :, 2 * hid + 128 :] = low
     over_dp("start", mine(grad_all), at(grad_all), 3)
+
+    @pl.when(s != nl - 1)
+    def _():
+        return_rows(1, s + 1, cross.at[lax.rem(s + 1, nl), p])
+
     over_dp("wait_recv", mine(grad_all), at(grad_all), 3)
     grads = grad_all[...].reshape(slots, 2 * hid + 256)
     act = act_all[...].reshape(slots, hid + 256)
     inv_slot = join(act[:, hid:])[:, :1]
     factor = join(grads[:, 2 * hid :])[:, :1]
-    back = lax.dot_general(
-        grads[:, :hid], wg[...], SECOND, preferred_element_type=F32
-    ) + lax.dot_general(grads[:, hid : 2 * hid], wu[...], SECOND, preferred_element_type=F32)
-    own_b[...] = (inv_slot * (gain_row * back) - a_ref[...] * factor).astype(BF16)
-
-    @pl.when(s != 0)
-    def _():
-        to_section(1, s, own_b, lax.rem(s + nl - 1, nl)).start()
-
-    return_rows(1, s, own_b[...].astype(F32))
+    for c in range(2):
+        columns = slice(c * half, (c + 1) * half)
+        back = lax.dot_general(
+            grads[:, :hid], wg[columns, :], SECOND, preferred_element_type=F32
+        ) + lax.dot_general(
+            grads[:, hid : 2 * hid], wu[columns, :], SECOND, preferred_element_type=F32
+        )
+        own_b[c] = (
+            inv_slot * (gain_row[:, columns] * back) - a_ref[:, columns] * factor
+        ).astype(BF16)
+
+        @pl.when(s != 0)
+        def _():
+            to_section(1, s, own_b.at[c], lax.rem(s + nl - 1, nl), c).start()
+
+    return_rows(1, s, own_b)
+    pl.when(s == nl - 1)(return_forward)
 
     normed = (a_ref[...] * inv_slot * gain_row).astype(BF16)
     step_w = 256 if dsl % 256 == 0 else 128
-    stores = []
     for start in range(0, dsl, step_w):
         left = normed[:, start : start + step_w]
         for out, lo in ((wg, 0), (wu, hid)):
             out[start : start + step_w, :] = lax.dot_general(
                 left, grads[:, lo : lo + hid], FIRST, preferred_element_type=F32
             ).astype(BF16)
-    stores.append(pltpu.make_async_copy(wg, out_g, store_sem.at[2]))
-    stores.append(pltpu.make_async_copy(wu, out_u, store_sem.at[3]))
-    stores[0].start()
-    stores[1].start()
     step_h = 256 if hid % 256 == 0 else 128
     slot_grad = (r_slot * g_ref[...]).astype(BF16)
     for start in range(0, hid, step_h):
         wd[start : start + step_h, :] = lax.dot_general(
             act[:, start : start + step_h], slot_grad, FIRST, preferred_element_type=F32
         ).astype(BF16)
-    stores.append(pltpu.make_async_copy(wd, out_d, store_sem.at[4]))
-    stores[2].start()
 
     pl.when(s == nl - 1)(finish_forward)
 
@@ -447,8 +506,6 @@
         return 0
 
     lax.fori_loop(0, nl - s, finish_backward, 0)
-    store_b = pltpu.make_async_copy(cot, out_b, store_sem.at[1])
-    store_b.start()
 
     dispatch_wait(0, True)
     dispatch_wait(1, True)
@@ -464,7 +521,8 @@
 
         @pl.when(s != nl - 1)
         def _():
-            to_section(0, layer, cross.at[layer, p], lax.rem(s + 1, nl)).wait_send()
+            for c in range(2):
+                to_section(0, layer, cross.at[layer, p, c], lax.rem(s + 1, nl), c).wait_send()
 
         return 0
 
@@ -475,7 +533,10 @@
 
         @pl.when((s != 0) & (layer != s))
         def _():
-            to_section(1, layer, cross.at[layer, p], lax.rem(s + nl - 1, nl)).wait_send()
+            for c in range(2):
+                to_section(
+                    1, layer, cross.at[layer, p, c], lax.rem(s + nl - 1, nl), c
+                ).wait_send()
 
         return 0
 
@@ -483,18 +544,27 @@
 
     @pl.when(s != 0)
     def _():
-        to_section(1, s, own_b, lax.rem(s + nl - 1, nl)).wait_send()
+        for c in range(2):
+            to_section(1, s, own_b.at[c], lax.rem(s + nl - 1, nl), c).wait_send()
 
     def drain_share(layer, _):
-        share(layer, "wait_send")
+        for c in range(2):
+            share(layer, "wait_send", c)
         return 0
 
     lax.fori_loop(0, s, drain_share, 0)
     lax.fori_loop(s + 1, nl, drain_share, 0)
-    for copy in stores:
+
+
+def write_out(*refs):
+    count = (len(refs) - 1) // 2
+    copies = [
+        pltpu.make_async_copy(refs[i], refs[count + i], refs[-1].at[i]) for i in range(count)
+    ]
+    for copy in copies:
+        copy.start()
+    for copy in copies:
         copy.wait()
-    store_f.wait()
-    store_b.wait()
 
 
 def local(
@@ -516,18 +586,16 @@
     results = pl.pallas_call(
         functools.partial(kernel, nz, nl, ne),
         out_shape=(
-            out((toks, width)), out((toks, width)), out((dsl, hid)), out((dsl, hid)),
-            out((hid, dsl)),
+            vm((toks, width), BF16), vm((toks, width), BF16), vm((dsl, hid), BF16),
+            vm((dsl, hid), BF16), vm((hid, dsl), BF16),
         ),
         in_specs=[anywhere, anywhere, vmem, vmem, vmem, smem, anywhere, anywhere, anywhere],
-        out_specs=(anywhere,) * 5,
+        out_specs=(vmem,) * 5,
         scratch_shapes=[
-            vm((toks, width), BF16), vm((toks, width), BF16),
-            vm((dsl, hid), BF16), vm((dsl, hid), BF16), vm((hid, dsl), BF16),
             vm((2, nb, 2 * CAP, half), BF16), vm((2, nb, 2 * CAP, half), BF16),
-            vm((rows, 256), F32), vm((nb, rows, 256), F32),
+            vm((rows, 128), F32),
             vm((nl, nb, rows, 128), F32),
-            vm((nl, ne, slots, dsl), BF16), vm((slots, dsl), BF16),
+            vm((nl, ne, 2, slots, half), BF16), vm((2, slots, half), BF16),
             vm((2, nl, nb, 2 * CAP, half), BF16), vm((2, nl, nb, 2 * CAP, half), BF16),
             vm((slots, dsl), F32), vm((slots, dsl), F32),
             vm((slots, 2 * hid + 256), BF16), vm((nz, rows, 2 * hid + 256), BF16),
@@ -535,20 +603,28 @@
             vm((slots, hid), BF16), vm((nz, rows, hid), BF16),
             vm((nz, rows, 2 * hid + 256), BF16),
             vm((rows, hid), F32), vm((rows, hid), F32), vm((rows, 128), F32),
-            dma((5,)), dma((5,)),
+            dma((5,)),
             dma((2, nb)), dma((2, nb)), dma((nb,)), dma((nb,)),
             dma((nl,)), dma((nl,)), dma((4, nz)), dma((4, nz)),
-            dma((2, nl)), dma((2, nl)), dma((nl, ne)), dma((nl, ne)),
+            dma((2, nl, 2)), dma((2, nl, 2)), dma((nl, ne, 2)), dma((nl, ne, 2)),
             dma((2, nl, nb)), dma((2, nl, nb)),
         ],
         compiler_params=pltpu.CompilerParams(
-            collective_id=0, has_side_effects=True, vmem_limit_bytes=58 * 2**20
+            collective_id=0, has_side_effects=True, vmem_limit_bytes=50 * 2**20
         ),
     )(
-        tokens, cotangent, norm_gain, route_gates[0], expert_ids[0], expert_map,
+        tokens, cotangent, norm_gain, jnp.transpose(route_gates, (2, 0, 1)),
+        jnp.transpose(expert_ids, (2, 0, 1)), expert_map,
         w_gate[0, 0], w_up[0, 0], w_down[0, 0],
     )
-    layer_out, input_grad, gate, up, down = results
+    layer_out, input_grad, gate, up, down = pl.pallas_call(
+        write_out,
+        out_shape=tuple(out(r.shape) for r in results),
+        in_specs=[anywhere] * 5,
+        out_specs=(anywhere,) * 5,
+        scratch_shapes=[dma((5,))],
+        compiler_params=pltpu.CompilerParams(vmem_limit_bytes=2**20),
+    )(*[pltpu.with_memory_space_constraint(r, pltpu.VMEM) for r in results])
     return layer_out[None], input_grad[None], gate[None, None], up[None, None], down[None, None]
 
 

time: 194 us -> 161 us (0.83)
  Pallas kernels: 180 us -> 160 us
  local copies, waits for them, and re-layouts: 13.2 us -> 0 us
    pallas_call x1 -> x2, Pallas kernels: 180 us -> 160 us  [the longest x1 157 us: local(): pl.pallas_call(functools.partial(kernel, nz, nl, ne), out_shape=(vm((toks...]
    unnamed x15 -> x0, local copies, waits for them, and re-layouts: 13.2 us -> none
where the time goes in v2:
time: 161 us
  Pallas kernels  160 us (99%)
    pallas_call x1, Pallas kernels, local(): pl.pallas_call(functools.partial(kernel, nz, nl, ne), out_shape=(vm((toks...  157 us
    pallas_call x1, Pallas kernels, local(): pl.pallas_call(write_out, out_shape=tuple((out(r.shape) for r in results)...  3.42 us

profile of v2, /device:TPU:0, one launch (start us, length us, event | category | flops | bytes accessed | tf_op | source)
XLA Modules:
  0.0 161.0 jit_solution(3236252135488674254)
XLA Ops:
  0.6 156.9 %shard_map.128 = (bf16[128,5120]{1,0:T(8,128)(2,1)S(1)}, bf16[128,5120]{1,0:T(8,128)(2,1)S(1)}, bf16[1280,768]{1,0:T(8,128)(2,1)S(1)}, bf16[1280,768]{1,0:T(8,128)(2,1)S(1)}, bf16[768,1280]{1,0:T(8,128)(2,1)S(1)}) custom-call(bf16[128,5120]{1,0:T(8,128)(2,1)} %tok_in.1, bf16[128,5120]{1,0:T(8,128)(2,1)} %cot_in.1, f32[1,5120]{1,0:T(1,128)} %gain.1, ...), custom_call_target="tpu_custom_call" | custom-call | tf_op jit(solution)/shard_map/pallas_call | solution.py:586
  157.6 3.4 %shard_map.129 = (bf16[128,5120]{1,0:T(8,128)(2,1)}, bf16[128,5120]{1,0:T(8,128)(2,1)}, bf16[1280,768]{1,0:T(8,128)(2,1)}, bf16[1280,768]{1,0:T(8,128)(2,1)}, bf16[768,1280]{1,0:T(8,128)(2,1)}) custom-call(bf16[128,5120]{1,0:T(8,128)(2,1)S(1)} %get-tuple-element.15.refs_0_, bf16[128,5120]{1,0:T(8,128)(2,1)S(1)} %get-tuple-element.16.refs_1_, ...), custom_call_target="tpu_custom_call" | custom-call | tf_op jit(solution)/shard_map/pallas_call | solution.py:620

commit v3 on v2

--- a/solution.py
+++ b/solution.py
@@ -17,13 +17,14 @@
 
 
 def split(value):
-    high = value.astype(BF16)
-    return high, (value - high.astype(F32)).astype(BF16)
-
-
-def join(ref_value):
-    wide = ref_value.astype(F32)
-    return wide[:, :128] + wide[:, 128:]
+    high = value.astype(BF16).astype(F32)
+    lane = lax.broadcasted_iota(jnp.int32, (value.shape[0], 128), 1)
+    return jnp.where(lane < TID, high, value - high).astype(BF16)
+
+
+def join(value):
+    wide = value.astype(F32)
+    return wide[:, :1] + wide[:, TID : TID + 1]
 
 
 def kernel(
@@ -31,7 +32,8 @@
     tok_in, cot_in, gain, gates, ids, emap, wg_in, wu_in, wd_in,
     tok, cot, wg, wu, wd,
     d_send, d_recv, m_send, idsall, cross, own_b, r_send, r_recv,
-    a_ref, g_ref, part, part_in, act_all, hpart, hpart_in, grad_all,
+    a_ref, g_ref, back_ref, part, part_in, part_u, part_u_in, act_all, hpart, hpart_in,
+    grad_all, grad_u,
     gp_ref, up_ref, inv_ref,
     load_sem, d_ss, d_rs, m_ss, m_rs, i_ss, i_rs, c_ss, c_rs,
     f_ss, f_rs, x_ss, x_rs, r_ss, r_rs,
@@ -342,33 +344,32 @@
     square = jnp.sum(wide * wide, axis=1, keepdims=True)
     loads[2].wait()
     part[:, :hid] = jnp.dot(x, wg[...], preferred_element_type=F32).astype(BF16)
+    part[:, hid:] = split(square)
+    over_dp("start", block(part), at(part_in), 0)
     loads[3].wait()
-    part[:, hid : 2 * hid] = jnp.dot(x, wu[...], preferred_element_type=F32).astype(BF16)
-    high, low = split(jnp.broadcast_to(square, (slots, 128)))
-    part[:, 2 * hid : 2 * hid + 128] = high
-    part[:, 2 * hid + 128 :] = low
-    over_dp("start", block(part), at(part_in), 0)
+    part_u[...] = jnp.dot(x, wu[...], preferred_element_type=F32).astype(BF16)
+    over_dp("start", block(part_u), at(part_u_in), 4)
     part_in[z] = part[pl.ds(pl.multiple_of(z * rows, 16), rows)]
+    part_u_in[z] = part_u[pl.ds(pl.multiple_of(z * rows, 16), rows)]
     pl.when(s == 0)(meta_settle)
     over_dp("wait_recv", block(part), at(part_in), 0)
     total = part_in[0].astype(F32)
     for i in range(1, nz):
         total = total + part_in[i].astype(F32)
-    inv = lax.rsqrt(join(total[:, 2 * hid :])[:, :1] / width + EPS)
+    inv = lax.rsqrt(join(total[:, hid:]) / width + EPS)
     gate_pre = total[:, :hid] * inv
-    up_pre = total[:, hid : 2 * hid] * inv
+    scaled = gate_pre * jax.nn.sigmoid(gate_pre)
+    over_dp("wait_recv", block(part_u), at(part_u_in), 4)
+    total = part_u_in[0].astype(F32)
+    for i in range(1, nz):
+        total = total + part_u_in[i].astype(F32)
+    up_pre = total * inv
+    act_all[z, :, :hid] = (scaled * up_pre).astype(BF16)
+    act_all[z, :, hid:] = split(inv)
+    over_dp("start", mine(act_all), at(act_all), 1)
     gp_ref[...] = gate_pre
     up_ref[...] = up_pre
     inv_ref[...] = jnp.broadcast_to(inv, (rows, 128))
-    act_all[z, :, :hid] = (gate_pre * jax.nn.sigmoid(gate_pre) * up_pre).astype(BF16)
-    high, low = split(inv_ref[...])
-    act_all[z, :, hid : hid + 128] = high
-    act_all[z, :, hid + 128 :] = low
-    over_dp("start", mine(act_all), at(act_all), 1)
-
-    @pl.when(s == 0)
-    def _():
-        cot_settle()
 
     @pl.when(s != nl - 1)
     def _():
@@ -376,7 +377,7 @@
 
     r_slot = own_meta()[:, 0:1]
     over_dp("wait_recv", mine(act_all), at(act_all), 1)
-    act = act_all[...].reshape(slots, hid + 256)
+    act = act_all[...].reshape(slots, hid + 128)
     for c in range(2):
         out_rows = r_slot * jnp.dot(
             act[:, :hid], wd[:, c * half : (c + 1) * half], preferred_element_type=F32
@@ -396,6 +397,7 @@
 
     @pl.when(s != nl - 1)
     def _():
+        pl.when(s == 0)(cot_settle)
         return_forward()
         dispatch_wait(1, False)
         g_ref[...] = unpack(1)
@@ -446,32 +448,36 @@
         hidden = hidden + hpart_in[i].astype(F32)
     gate_grad = (hidden * up_pre * sig * (1.0 + gate_pre * (1.0 - sig))).astype(BF16)
     up_grad = (hidden * gate_pre * sig).astype(BF16)
-    grad_all[z, :, :hid] = gate_grad
-    grad_all[z, :, hid : 2 * hid] = up_grad
     along = jnp.sum(
         gate_grad.astype(F32) * gate_pre + up_grad.astype(F32) * up_pre, axis=1, keepdims=True
     )
-    inv = inv_ref[...]
-    high, low = split(inv * inv * along / width)
-    grad_all[z, :, 2 * hid : 2 * hid + 128] = high
-    grad_all[z, :, 2 * hid + 128 :] = low
+    inv = inv_ref[:, :1]
+    grad_all[z, :, :hid] = gate_grad
+    grad_all[z, :, hid:] = split(inv * inv * along / width)
     over_dp("start", mine(grad_all), at(grad_all), 3)
-
-    @pl.when(s != nl - 1)
-    def _():
-        return_rows(1, s + 1, cross.at[lax.rem(s + 1, nl), p])
-
+    grad_u[z] = up_grad
+    over_dp("start", mine(grad_u), at(grad_u), 5)
+    act = act_all[...].reshape(slots, hid + 128)
+    inv_slot = join(act[:, hid:])
     over_dp("wait_recv", mine(grad_all), at(grad_all), 3)
-    grads = grad_all[...].reshape(slots, 2 * hid + 256)
-    act = act_all[...].reshape(slots, hid + 256)
-    inv_slot = join(act[:, hid:])[:, :1]
-    factor = join(grads[:, 2 * hid :])[:, :1]
+    grads = grad_all[...].reshape(slots, hid + 128)
+    factor = join(grads[:, hid:])
     for c in range(2):
         columns = slice(c * half, (c + 1) * half)
-        back = lax.dot_general(
+        back_ref[:, columns] = lax.dot_general(
             grads[:, :hid], wg[columns, :], SECOND, preferred_element_type=F32
-        ) + lax.dot_general(
-            grads[:, hid : 2 * hid], wu[columns, :], SECOND, preferred_element_type=F32
+        )
+    over_dp("wait_recv", mine(grad_u), at(grad_u), 5)
+    grads_u = grad_u[...].reshape(slots, hid)
+
+    def return_next():
+        return_rows(1, s + 1, cross.at[lax.rem(s + 1, nl), p])
+
+    pl.when(s == 0)(return_next)
+    for c in range(2):
+        columns = slice(c * half, (c + 1) * half)
+        back = back_ref[:, columns] + lax.dot_general(
+            grads_u, wu[columns, :], SECOND, preferred_element_type=F32
         )
         own_b[c] = (
             inv_slot * (gain_row[:, columns] * back) - a_ref[:, columns] * factor
@@ -481,6 +487,7 @@
         def _():
             to_section(1, s, own_b.at[c], lax.rem(s + nl - 1, nl), c).start()
 
+    pl.when((s != 0) & (s != nl - 1))(return_next)
     return_rows(1, s, own_b)
     pl.when(s == nl - 1)(return_forward)
 
@@ -488,9 +495,9 @@
     step_w = 256 if dsl % 256 == 0 else 128
     for start in range(0, dsl, step_w):
         left = normed[:, start : start + step_w]
-        for out, lo in ((wg, 0), (wu, hid)):
+        for out, right in ((wg, grads[:, :hid]), (wu, grads_u)):
             out[start : start + step_w, :] = lax.dot_general(
-                left, grads[:, lo : lo + hid], FIRST, preferred_element_type=F32
+                left, right, FIRST, preferred_element_type=F32
             ).astype(BF16)
     step_h = 256 if hid % 256 == 0 else 128
     slot_grad = (r_slot * g_ref[...]).astype(BF16)
@@ -515,6 +522,8 @@
     over_dp("wait_send", mine(act_all), at(act_all), 1)
     over_dp("wait_send", block(hpart), at(hpart_in), 2)
     over_dp("wait_send", mine(grad_all), at(grad_all), 3)
+    over_dp("wait_send", block(part_u), at(part_u_in), 4)
+    over_dp("wait_send", mine(grad_u), at(grad_u), 5)
 
     def drain_forward(layer, _):
         return_wait(0, layer, True)
@@ -597,15 +606,16 @@
             vm((nl, nb, rows, 128), F32),
             vm((nl, ne, 2, slots, half), BF16), vm((2, slots, half), BF16),
             vm((2, nl, nb, 2 * CAP, half), BF16), vm((2, nl, nb, 2 * CAP, half), BF16),
-            vm((slots, dsl), F32), vm((slots, dsl), F32),
-            vm((slots, 2 * hid + 256), BF16), vm((nz, rows, 2 * hid + 256), BF16),
-            vm((nz, rows, hid + 256), BF16),
+            vm((slots, dsl), F32), vm((slots, dsl), F32), vm((slots, dsl), F32),
+            vm((slots, hid + 128), BF16), vm((nz, rows, hid + 128), BF16),
             vm((slots, hid), BF16), vm((nz, rows, hid), BF16),
-            vm((nz, rows, 2 * hid + 256), BF16),
+            vm((nz, rows, hid + 128), BF16),
+            vm((slots, hid), BF16), vm((nz, rows, hid), BF16),
+            vm((nz, rows, hid + 128), BF16), vm((nz, rows, hid), BF16),
             vm((rows, hid), F32), vm((rows, hid), F32), vm((rows, 128), F32),
             dma((5,)),
             dma((2, nb)), dma((2, nb)), dma((nb,)), dma((nb,)),
-            dma((nl,)), dma((nl,)), dma((4, nz)), dma((4, nz)),
+            dma((nl,)), dma((nl,)), dma((6, nz)), dma((6, nz)),
             dma((2, nl, 2)), dma((2, nl, 2)), dma((nl, ne, 2)), dma((nl, ne, 2)),
             dma((2, nl, nb)), dma((2, nl, nb)),
         ],

time: 161 us -> 151 us (0.938)
  Pallas kernels: 160 us -> 150 us
    pallas_call x1, Pallas kernels: 157 us -> 147 us  [local(): pl.pallas_call(functools.partial(kernel, nz, nl, ne), out_shape=(vm((toks...]
where the time goes in v3:
time: 151 us
  Pallas kernels  150 us (99%)
    pallas_call x1, Pallas kernels, local(): pl.pallas_call(functools.partial(kernel, nz, nl, ne), out_shape=(vm((toks...  147 us
    pallas_call x1, Pallas kernels, local(): pl.pallas_call(write_out, out_shape=tuple((out(r.shape) for r in results)...  3.42 us

profile of v3, /device:TPU:0, one launch (start us, length us, event | category | flops | bytes accessed | tf_op | source)
XLA Modules:
  0.0 151.1 jit_solution(15823636948065643972)
XLA Ops:
  0.6 147.1 %shard_map.128 = (bf16[128,5120]{1,0:T(8,128)(2,1)S(1)}, bf16[128,5120]{1,0:T(8,128)(2,1)S(1)}, bf16[1280,768]{1,0:T(8,128)(2,1)S(1)}, bf16[1280,768]{1,0:T(8,128)(2,1)S(1)}, bf16[768,1280]{1,0:T(8,128)(2,1)S(1)}) custom-call(bf16[128,5120]{1,0:T(8,128)(2,1)} %tok_in.1, bf16[128,5120]{1,0:T(8,128)(2,1)} %cot_in.1, f32[1,5120]{1,0:T(1,128)} %gain.1, ...), custom_call_target="tpu_custom_call" | custom-call | tf_op jit(solution)/shard_map/pallas_call | solution.py:595
  147.7 3.4 %shard_map.129 = (bf16[128,5120]{1,0:T(8,128)(2,1)}, bf16[128,5120]{1,0:T(8,128)(2,1)}, bf16[1280,768]{1,0:T(8,128)(2,1)}, bf16[1280,768]{1,0:T(8,128)(2,1)}, bf16[768,1280]{1,0:T(8,128)(2,1)}) custom-call(bf16[128,5120]{1,0:T(8,128)(2,1)S(1)} %get-tuple-element.15.refs_0_, bf16[128,5120]{1,0:T(8,128)(2,1)S(1)} %get-tuple-element.16.refs_1_, ...), custom_call_target="tpu_custom_call" | custom-call | tf_op jit(solution)/shard_map/pallas_call | solution.py:630
